TPU v7x, 128 devices: a whole 4x4x4 slice. The times are simulated.
128 devices in a mesh: corr: 16 (over y, x), lc: 8 (over z, core).
Axes of the slice: x: 4, y: 4, z: 4, core: 2. Of those that a mesh axis runs over, the one named last changes fastest.
Arguments:
- density: float32 [4, 3, 2048, 1024], P(None, None, 'corr', 'lc'), may hold values from 0.002 to 0.16
- cap_code: int32 [4, 2048, 1024], P(None, 'corr', 'lc'), may hold values from 0 to 7
- jam_code: int32 [4, 2048, 1024], P(None, 'corr', 'lc'), may hold values from 0 to 3
- adjacency: int32 [3, 2048, 1024], P(None, 'corr', 'lc'), may hold values 0 or 1
- ramp_code: int32 [8, 4, 1024], P(None, None, 'lc'), may hold values from 0 to 7
- feed_a: int32 [1024], P('lc'), may hold values from 0 to 1023, each once
- feed_b: int32 [1024], P('lc'), may hold values from 0 to 1023, each once
- turn_share: float32 [1024], P('lc'), may hold values from 0.2 to 0.8
- priority: float32 [1024], P('lc'), may hold values from 0.2 to 0.8
- cap_table: float32 [8], replicated, may hold values from 0.1 to 0.25
- jam_table: float32 [4], replicated, may hold values from 0.8 to 1.2
- change_coef: float32 [3], replicated, may hold values from 0.05 to 0.2
Outputs:
- traffic: float32 [4, 3, 2048, 1024], P(None, None, 'corr', 'lc')
- queue_count: float32 [2048, 1024], P('corr', 'lc')
Inputs may be any that keep to these rules, and one draw needn't show every extreme that they name: `feed_a`: every corridor appears exactly once. `feed_b`: every corridor appears exactly once.
All inputs are finite; a program needn't handle non-finite values. No bound on the sum of `adjacency` on one device may be relied on, other than what follows from the above.
Results may differ from a plain program's by a relative error of at most 0.0001.
Values sent between devices are 32-bit elements; how exact they have to be, the bound alone decides.
No kernel may reach another device: no remote copies, remote signals or barrier semaphores. Data moves between devices by JAX's collectives and lax.ppermute only.
A program may use at most 64 MiB of HBM per device.

v0:
```python
import jax
import jax.numpy as jnp
from jax import lax
from jax.sharding import PartitionSpec as P

STEPS = 8


pce_weights = (1.0, 1.5, 2.5)
ramp_unit = 0.01
ramp_fraction = (0.56, 0.16, 0.08)


def carried_in(part, axis, combine, identity):
    place = lax.axis_index(axis)
    gathered = lax.all_gather(part, axis)
    state = jnp.zeros_like(part) + jnp.asarray(identity, part.dtype)

    def one(step, state):
        return combine(state, lax.dynamic_index_in_dim(gathered, step, 0, False))

    return lax.fori_loop(0, place, one, state)


def with_halo(block, sides, width):
    for axis, dim in sides:
        count = lax.axis_size(axis)
        forward = [(i, i + 1) for i in range(count - 1)]
        forward.append((count - 1, 0))
        backward = [(target, source) for source, target in forward]
        low = lax.ppermute(
            lax.slice_in_dim(block, block.shape[dim] - width, None, axis=dim), axis, forward
        )
        high = lax.ppermute(lax.slice_in_dim(block, 0, width, axis=dim), axis, backward)
        block = jnp.concatenate([low, block, high], axis=dim)
    return block


def lookup(codes, values):
    looked = jnp.zeros(codes.shape, values.dtype)
    for code_value in range(values.shape[0]):
        looked = looked + jnp.where(codes == code_value, values[code_value], 0.0)
    return looked


def pce_total(state):
    totals = state[:, 0] * pce_weights[0]
    for class_index in range(1, len(pce_weights)):
        totals = totals + state[:, class_index] * pce_weights[class_index]
    return totals


def cell_terms(state, totals, capacity, jam_cap, wave_speed):
    speeds = capacity / jnp.maximum(totals, 2.0 * capacity)
    demand = state * speeds[:, None]
    pce_demand = totals * speeds
    supply = jnp.maximum(jnp.minimum(capacity, wave_speed * (jam_cap - totals)), 0.0)
    return (demand, pce_demand, supply)


def middle(first_term, second_term, third_term):
    return jnp.maximum(
        jnp.minimum(first_term, second_term),
        jnp.minimum(jnp.maximum(first_term, second_term), third_term),
    )


def junction(take_a, take_b, supply, share_a, share_b):
    class_count = take_a.shape[1] - 1
    need_a = take_a[:, class_count]
    need_b = take_b[:, class_count]
    pass_a = jnp.minimum(need_a, middle(need_a, supply - need_b, share_a))
    pass_b = jnp.minimum(need_b, middle(need_b, supply - need_a, share_b))
    rate_a = pass_a / need_a
    rate_b = pass_b / need_b
    inflow = take_a[:, :class_count] * rate_a[:, None] + take_b[:, :class_count] * rate_b[:, None]
    spare = jnp.maximum(supply - pass_a - pass_b, 0.0)
    return (inflow, spare, rate_a, rate_b)


def ramp_inflow(ramp_row, spare):
    ramp_flow = jnp.minimum(ramp_row.astype(jnp.float32) * ramp_unit, spare)
    fractions = jnp.array(ramp_fraction, dtype=jnp.float32)
    return ramp_flow[:, None] * fractions[None, :, None]


def lane_change(state, change_rate):
    moving = change_rate * (state[:-1] - state[1:])
    zeros_row = jnp.zeros_like(state[:1])
    return state - jnp.concatenate([moving, zeros_row], 0) + jnp.concatenate([zeros_row, moving], 0)


def combine(earlier, later_part):
    return jnp.stack(
        [earlier[0] + later_part[0], jnp.minimum(earlier[1], earlier[0] + later_part[1])]
    )


def prefix_carry(segment_stats):
    identity = jnp.stack(
        [jnp.zeros_like(segment_stats[0]), jnp.full_like(segment_stats[1], jnp.inf)]
    )
    carried = carried_in(segment_stats, "corr", combine, identity)
    return carried


def on_device(
    density,
    cap_code,
    jam_code,
    adjacency,
    ramp_code,
    feed_a,
    feed_b,
    turn_share,
    priority,
    cap_table,
    jam_table,
    change_coef,
):
    lane_count, class_count, cell_count, local_width = density.shape
    row_index = lax.axis_index("corr")
    row_count = lax.axis_size("corr")
    head_row = row_index == 0
    tail_row = row_index == row_count - 1
    capacity = lookup(cap_code, cap_table)
    jam_cap = lookup(jam_code, jam_table)
    critical = 2.0 * capacity
    wave_speed = capacity / (jam_cap - critical)
    change_rate = change_coef[None, :, None, None] * adjacency.astype(jnp.float32)[:, None]
    state = density
    totals = pce_total(state)
    accumulated = jnp.zeros((cell_count, local_width), jnp.float32)
    for step_index in range(STEPS):
        demand, pce_demand, supply = cell_terms(state, totals, capacity, jam_cap, wave_speed)
        packed = jnp.concatenate([demand, pce_demand[:, None], supply[:, None]], 1)
        padded = with_halo(packed, (("corr", 2),), 1)
        left_rim = padded[:, :, 0]
        right_rim = padded[:, :, cell_count + 1]
        next_supply = jnp.concatenate([supply[:, 1:], right_rim[:, None, class_count + 1]], 1)
        ratios = jnp.minimum(pce_demand, next_supply) / pce_demand
        out_flux = demand * ratios[:, None]
        left_pce = left_rim[:, class_count]
        entering = (
            left_rim[:, :class_count] * (jnp.minimum(left_pce, supply[:, 0]) / left_pce)[:, None]
        )
        own_ends = jnp.concatenate([demand[:, :, -1], pce_demand[:, None, -1]], 1)
        end_vals = jnp.where(head_row, left_rim[:, : class_count + 1], own_ends)
        head_supply = jnp.where(head_row, supply[:, 0], right_rim[:, class_count + 1])
        part_a = turn_share * end_vals
        part_b = (1.0 - turn_share) * end_vals
        share_a = priority * head_supply
        share_b = (1.0 - priority) * head_supply
        end_pack = lax.all_gather(jnp.stack([part_a, part_b]), "lc", axis=3, tiled=True)
        take_a = jnp.take(end_pack[0], feed_a, axis=2)
        take_b = jnp.take(end_pack[1], feed_b, axis=2)
        inflow, spare, rate_a, rate_b = junction(take_a, take_b, head_supply, share_a, share_b)
        spread_a = jnp.zeros((lane_count, end_pack.shape[3]), jnp.float32).at[:, feed_a].set(rate_a)
        spread_b = jnp.zeros((lane_count, end_pack.shape[3]), jnp.float32).at[:, feed_b].set(rate_b)
        returned = lax.psum_scatter(
            jnp.stack([spread_a, spread_b]), "lc", scatter_dimension=2, tiled=True
        )
        back_a = returned[0]
        back_b = returned[1]
        arriving = inflow + ramp_inflow(ramp_code[step_index], spare)
        leaving = (
            part_a[:, :class_count] * back_a[:, None] + part_b[:, :class_count] * back_b[:, None]
        )
        in_flux = jnp.concatenate(
            [jnp.where(head_row, arriving, entering)[:, :, None], out_flux[:, :, :-1]], 2
        )
        out_final = jnp.concatenate(
            [out_flux[:, :, :-1], jnp.where(tail_row, leaving, out_flux[:, :, -1])[:, :, None]], 2
        )
        state = state + in_flux - out_final
        state = lane_change(state, change_rate)
        totals = pce_total(state)
        excess = jnp.sum(totals - critical, 0) * 0.25
        local_sum = jnp.cumsum(excess, 0)
        local_low = lax.cummin(local_sum, axis=0)
        segment_stats = jnp.stack([local_sum[-1], local_low[-1]])
        carried = prefix_carry(segment_stats)
        running = carried[0] + local_sum
        lowest = jnp.minimum(jnp.minimum(carried[1], carried[0] + local_low), 0.0)
        accumulated = accumulated + (running - lowest)
    return (state, accumulated / float(STEPS * cell_count * row_count))


def solution(mesh):
    placed = (
        P(None, None, "corr", "lc"),
        P(None, "corr", "lc"),
        P(None, "corr", "lc"),
        P(None, "corr", "lc"),
        P(None, None, "lc"),
        P("lc"),
        P("lc"),
        P("lc"),
        P("lc"),
        P(),
        P(),
        P(),
    )
    return jax.shard_map(
        on_device,
        mesh=mesh,
        in_specs=placed,
        out_specs=(P(None, None, "corr", "lc"), P("corr", "lc")),
        check_vma=False,
    )
```

profile of v0, /device:TPU:0, one launch (start us, length us, event | category | flops | bytes accessed | tf_op | source)
XLA Modules:
  0.0 764.8 jit_solution(16078061449665464926)
XLA Ops:
  11.5 9.5 %minimum_maximum_fusion.7 = (f32[4,128,128]{2,0,1:T(4,128)S(1)}, f32[4,128,128]{2,0,1:T(4,128)S(1)}) fusion(f32[4,128,128]{2,1,0:T(8,128)S(1)} %add_bitcast_fusion, f32[]{:T(128)} %bitcast.45, f32[]{:T(128)} %bitcast.44, f32[]{:T(128)} %bitcast.43, f32[]{:T(128)} %bitcast.42, s32[4,128,128]{2,1,0:T(8,128)} %param.40, f32[]{:T(128)} %bitcast.39, ...), kind=kLoop, calls=%fused_computation.239 | loop fusion | flops 2686976 | bytes 1310768 | tf_op jit(solution)/shard_map/max | solution.py:57
  23.1 3.8 collective-permute-start.1
  29.1 12.9 %all_gather.72 = f32[2,4,4,1024]{3,2,1,0:T(4,128)S(1)} all-gather(f32[2,4,4,128]{3,2,1,0:T(4,128)S(1)} %pad_maximum_fusion.16), channel_id=1, replica_groups=mesh['corr'=16,'lc'=8] {'lc'}, dimensions={3}, use_global_device_ids=true | all-gather | bytes 147456 | tf_op jit(solution)/shard_map/all_gather | solution.py:154
  44.4 2.4 gather_fusion
  61.9 24.6 %reduce-scatter.25.cloned.1.call-done = f32[128,8]{1,0:T(8,128)} async-done(((f32[1024,8]{1,0:T(8,128)}), f32[128,8]{1,0:T(8,128)}) %reduce-scatter.25.cloned.1.call-update) | async-done | bytes 4112
  89.0 3.1 copy_multiply_fusion.7
  94.9 3.9 collective-permute-start.3
  100.0 11.3 %all_gather.73 = f32[2,4,4,1024]{3,2,1,0:T(4,128)S(1)} all-gather(f32[2,4,4,128]{3,2,1,0:T(4,128)S(1)} %pad_maximum_fusion.17), channel_id=1, replica_groups=mesh['corr'=16,'lc'=8] {'lc'}, dimensions={3}, use_global_device_ids=true | all-gather | bytes 147456 | tf_op jit(solution)/shard_map/all_gather | solution.py:154
  113.0 2.5 gather_fusion.2
  117.4 2.5 gather_fusion.3
  127.4 27.0 %reduce-scatter.27.cloned.1.call-done = f32[128,8]{1,0:T(8,128)} async-done(((f32[1024,8]{1,0:T(8,128)}), f32[128,8]{1,0:T(8,128)}) %reduce-scatter.27.cloned.1.call-update) | async-done | bytes 4112
  156.0 3.1 copy_multiply_fusion.6
  162.4 3.9 collective-permute-start.5
  167.5 11.3 %all_gather.74 = f32[2,4,4,1024]{3,2,1,0:T(4,128)S(1)} all-gather(f32[2,4,4,128]{3,2,1,0:T(4,128)S(1)} %pad_maximum_fusion.18), channel_id=1, replica_groups=mesh['corr'=16,'lc'=8] {'lc'}, dimensions={3}, use_global_device_ids=true | all-gather | bytes 147456 | tf_op jit(solution)/shard_map/all_gather | solution.py:154
  180.5 2.5 gather_fusion.4
  184.8 2.5 gather_fusion.5
  199.2 25.2 %reduce-scatter.29.cloned.1.call-done = f32[128,8]{1,0:T(8,128)} async-done(((f32[1024,8]{1,0:T(8,128)}), f32[128,8]{1,0:T(8,128)}) %reduce-scatter.29.cloned.1.call-update) | async-done | bytes 4112
  227.0 3.1 copy_multiply_fusion.5
  233.8 3.9 collective-permute-start.7
  239.4 11.7 %all_gather.75 = f32[2,4,4,1024]{3,2,1,0:T(4,128)S(1)} all-gather(f32[2,4,4,128]{3,2,1,0:T(4,128)S(1)} %pad_maximum_fusion.19), channel_id=1, replica_groups=mesh['corr'=16,'lc'=8] {'lc'}, dimensions={3}, use_global_device_ids=true | all-gather | bytes 147456 | tf_op jit(solution)/shard_map/all_gather | solution.py:154
  252.9 2.4 gather_fusion.6
  257.1 2.4 gather_fusion.7
  267.1 26.0 %reduce-scatter.31.cloned.1.call-done = f32[128,8]{1,0:T(8,128)} async-done(((f32[1024,8]{1,0:T(8,128)}), f32[128,8]{1,0:T(8,128)}) %reduce-scatter.31.cloned.1.call-update) | async-done | bytes 4112
  294.7 3.1 copy_multiply_fusion.4
  301.6 3.9 collective-permute-start.9
  307.1 11.3 %all_gather.76 = f32[2,4,4,1024]{3,2,1,0:T(4,128)S(1)} all-gather(f32[2,4,4,128]{3,2,1,0:T(4,128)S(1)} %pad_maximum_fusion.20), channel_id=1, replica_groups=mesh['corr'=16,'lc'=8] {'lc'}, dimensions={3}, use_global_device_ids=true | all-gather | bytes 147456 | tf_op jit(solution)/shard_map/all_gather | solution.py:154
  334.5 25.8 %reduce-scatter.33.cloned.1.call-done = f32[128,8]{1,0:T(8,128)} async-done(((f32[1024,8]{1,0:T(8,128)}), f32[128,8]{1,0:T(8,128)}) %reduce-scatter.33.cloned.1.call-update) | async-done | bytes 4112
  362.0 3.1 copy_multiply_fusion.3
  368.8 3.9 collective-permute-start.11
  374.3 11.3 %all_gather.77 = f32[2,4,4,1024]{3,2,1,0:T(4,128)S(1)} all-gather(f32[2,4,4,128]{3,2,1,0:T(4,128)S(1)} %pad_maximum_fusion.21), channel_id=1, replica_groups=mesh['corr'=16,'lc'=8] {'lc'}, dimensions={3}, use_global_device_ids=true | all-gather | bytes 147456 | tf_op jit(solution)/shard_map/all_gather | solution.py:154
  401.5 26.0 %reduce-scatter.35.cloned.1.call-done = f32[128,8]{1,0:T(8,128)} async-done(((f32[1024,8]{1,0:T(8,128)}), f32[128,8]{1,0:T(8,128)}) %reduce-scatter.35.cloned.1.call-update) | async-done | bytes 4112
  429.2 3.1 copy_multiply_fusion.2
  436.0 3.9 collective-permute-start.13
  441.6 11.5 %all_gather.78 = f32[2,4,4,1024]{3,2,1,0:T(4,128)S(1)} all-gather(f32[2,4,4,128]{3,2,1,0:T(4,128)S(1)} %pad_maximum_fusion.22), channel_id=1, replica_groups=mesh['corr'=16,'lc'=8] {'lc'}, dimensions={3}, use_global_device_ids=true | all-gather | bytes 147456 | tf_op jit(solution)/shard_map/all_gather | solution.py:154
  469.0 26.0 %reduce-scatter.37.cloned.1.call-done = f32[128,8]{1,0:T(8,128)} async-done(((f32[1024,8]{1,0:T(8,128)}), f32[128,8]{1,0:T(8,128)}) %reduce-scatter.37.cloned.1.call-update) | async-done | bytes 4112
  496.7 3.1 copy_multiply_fusion.1
  503.5 3.9 collective-permute-start.15
  509.0 11.3 %all_gather.79 = f32[2,4,4,1024]{3,2,1,0:T(4,128)S(1)} all-gather(f32[2,4,4,128]{3,2,1,0:T(4,128)S(1)} %pad_maximum_fusion.23), channel_id=1, replica_groups=mesh['corr'=16,'lc'=8] {'lc'}, dimensions={3}, use_global_device_ids=true | all-gather | bytes 147456 | tf_op jit(solution)/shard_map/all_gather | solution.py:154
  536.5 26.0 %reduce-scatter.39.cloned.1.call-done = f32[128,8]{1,0:T(8,128)} async-done(((f32[1024,8]{1,0:T(8,128)}), f32[128,8]{1,0:T(8,128)}) %reduce-scatter.39.cloned.1.call-update) | async-done | bytes 4112
  565.7 3.0 subtract_reduce_fusion.6
  573.2 23.3 %all-gather.8 = f32[16,2,128]{2,1,0:T(2,128)S(1)} all-gather(f32[1,2,128]{2,1,0:T(2,128)S(1)} %maximum_bitcast_fusion), channel_id=2, replica_groups=mesh['corr'=16,'lc'=8] {'corr'}, dimensions={0}, use_global_device_ids=true | all-gather | bytes 17408 | tf_op jit(solution)/shard_map/all_gather | solution.py:16
  596.6 23.4 %all-gather.9 = f32[16,2,128]{2,1,0:T(2,128)S(1)} all-gather(f32[1,2,128]{2,1,0:T(2,128)S(1)} %maximum_bitcast_fusion.1), channel_id=3, replica_groups=mesh['corr'=16,'lc'=8] {'corr'}, dimensions={0}, use_global_device_ids=true | all-gather | bytes 17408 | tf_op jit(solution)/shard_map/all_gather | solution.py:16
  620.0 22.1 %all-gather.10 = f32[16,2,128]{2,1,0:T(2,128)S(1)} all-gather(f32[1,2,128]{2,1,0:T(2,128)S(1)} %maximum_bitcast_fusion.2), channel_id=4, replica_groups=mesh['corr'=16,'lc'=8] {'corr'}, dimensions={0}, use_global_device_ids=true | all-gather | bytes 17408 | tf_op jit(solution)/shard_map/all_gather | solution.py:16
  642.1 23.4 %all-gather.11 = f32[16,2,128]{2,1,0:T(2,128)S(1)} all-gather(f32[1,2,128]{2,1,0:T(2,128)S(1)} %maximum_bitcast_fusion.3), channel_id=5, replica_groups=mesh['corr'=16,'lc'=8] {'corr'}, dimensions={0}, use_global_device_ids=true | all-gather | bytes 17408 | tf_op jit(solution)/shard_map/all_gather | solution.py:16
  665.6 22.1 %all-gather.12 = f32[16,2,128]{2,1,0:T(2,128)S(1)} all-gather(f32[1,2,128]{2,1,0:T(2,128)S(1)} %maximum_bitcast_fusion.4), channel_id=6, replica_groups=mesh['corr'=16,'lc'=8] {'corr'}, dimensions={0}, use_global_device_ids=true | all-gather | bytes 17408 | tf_op jit(solution)/shard_map/all_gather | solution.py:16
  687.7 23.4 %all-gather.13 = f32[16,2,128]{2,1,0:T(2,128)S(1)} all-gather(f32[1,2,128]{2,1,0:T(2,128)S(1)} %maximum_bitcast_fusion.5), channel_id=7, replica_groups=mesh['corr'=16,'lc'=8] {'corr'}, dimensions={0}, use_global_device_ids=true | all-gather | bytes 17408 | tf_op jit(solution)/shard_map/all_gather | solution.py:16
  711.2 22.1 %all-gather.14 = f32[16,2,128]{2,1,0:T(2,128)S(1)} all-gather(f32[1,2,128]{2,1,0:T(2,128)S(1)} %maximum_bitcast_fusion.6), channel_id=8, replica_groups=mesh['corr'=16,'lc'=8] {'corr'}, dimensions={0}, use_global_device_ids=true | all-gather | bytes 17408 | tf_op jit(solution)/shard_map/all_gather | solution.py:16
  733.3 23.4 %all-gather.15 = f32[16,2,128]{2,1,0:T(2,128)S(1)} all-gather(f32[1,2,128]{2,1,0:T(2,128)S(1)} %maximum_bitcast_fusion.7), channel_id=9, replica_groups=mesh['corr'=16,'lc'=8] {'corr'}, dimensions={0}, use_global_device_ids=true | all-gather | bytes 17408 | tf_op jit(solution)/shard_map/all_gather | solution.py:16
  (761 shorter events, 181.6 us)
Async XLA Ops:
  7.2 79.3 %reduce-scatter.25.cloned.1.call-start = ((), (), s32[]{:S(2)}) async-start(), calls=%async_computation.8 | async-start | bytes 589824
  21.5 7.1 collective-permute-start
  23.1 27.9 %collective-permute-start.1 = (f32[4,5,1,128]{3,2,1,0:T(1,128)S(1)}, f32[4,5,1,128]{3,2,1,0:T(1,128)S(1)}, u32[]{:S(2)}, u32[]{:S(2)}) collective-permute-start(f32[4,5,1,128]{3,2,1,0:T(1,128)S(1)} %get-tuple-element.392), channel_id=1, source_target_pairs={{8,0},{16,8},{24,16},{32,24},{40,32},{48,40},{56,48},{64,56},{72,6... | collective-permute-start | bytes 30728 | tf_op jit(solution)/shard_map/ppermute | solution.py:34
  27.0 26.5 %copy-start.80 = (s32[128]{0:T(128)}, s32[128]{0:T(128)S(1)}, u32[]{:S(2)}) copy-start(s32[128]{0:T(128)S(1)} %compare_select_fusion.1) | copy-start | bytes 1540
  58.0 29.7 %copy-start.20 = (f32[4,4,128]{0,2,1:T(8,128)S(1)}, f32[4,4,128]{0,2,1:T(8,128)}, u32[]{:S(2)}) copy-start(f32[4,4,128]{0,2,1:T(8,128)} %copy-done.19) | copy-start | bytes 24580
  58.0 96.4 %reduce-scatter.27.cloned.1.call-start = ((), (), s32[]{:S(2)}) async-start(), calls=%async_computation.9 | async-start | bytes 589824
  61.7 26.2 %copy-start.58 = (f32[3]{0:T(128)S(1)}, f32[3]{0:T(128)}, u32[]{:S(2)}) copy-start(f32[3]{0:T(128)} %param.49) | copy-start | bytes 40
  92.3 7.1 collective-permute-start.2
  94.9 25.1 %collective-permute-start.3 = (f32[4,5,1,128]{3,2,1,0:T(1,128)S(1)}, f32[4,5,1,128]{3,2,1,0:T(1,128)S(1)}, u32[]{:S(2)}, u32[]{:S(2)}) collective-permute-start(f32[4,5,1,128]{3,2,1,0:T(1,128)S(1)} %get-tuple-element.390), channel_id=1, source_target_pairs={{8,0},{16,8},{24,16},{32,24},{40,32},{48,40},{56,48},{64,56},{72,6... | collective-permute-start | bytes 30728 | tf_op jit(solution)/shard_map/ppermute | solution.py:34
  125.9 29.6 %copy-start.41 = (f32[4,4,128]{0,2,1:T(8,128)S(1)}, f32[4,4,128]{0,2,1:T(8,128)}, u32[]{:S(2)}) copy-start(f32[4,4,128]{0,2,1:T(8,128)} %copy-done.40) | copy-start | bytes 24580
  125.9 98.5 %reduce-scatter.29.cloned.1.call-start = ((), (), s32[]{:S(2)}) async-start(), calls=%async_computation.10 | async-start | bytes 589824
  159.9 7.0 collective-permute-start.4
  162.4 25.1 %collective-permute-start.5 = (f32[4,5,1,128]{3,2,1,0:T(1,128)}, f32[4,5,1,128]{3,2,1,0:T(1,128)S(1)}, u32[]{:S(2)}, u32[]{:S(2)}) collective-permute-start(f32[4,5,1,128]{3,2,1,0:T(1,128)} %get-tuple-element.388), channel_id=1, source_target_pairs={{8,0},{16,8},{24,16},{32,24},{40,32},{48,40},{56,48},{64,56},{72,6... | collective-permute-start | bytes 30728 | tf_op jit(solution)/shard_map/ppermute | solution.py:34
  195.9 29.5 %copy-start.22 = (f32[4,4,128]{0,2,1:T(8,128)S(1)}, f32[4,4,128]{0,2,1:T(8,128)}, u32[]{:S(2)}) copy-start(f32[4,4,128]{0,2,1:T(8,128)} %copy-done.21) | copy-start | bytes 24580
  195.9 97.1 %reduce-scatter.31.cloned.1.call-start = ((), (), s32[]{:S(2)}) async-start(), calls=%async_computation.11 | async-start | bytes 589824
  199.0 27.7 %copy-start.59 = (f32[3]{0:T(128)S(1)}, f32[3]{0:T(128)}, u32[]{:S(2)}) copy-start(f32[3]{0:T(128)} %param.49) | copy-start | bytes 40
  230.3 7.5 collective-permute-start.6
  233.8 25.8 %collective-permute-start.7 = (f32[4,5,1,128]{3,2,1,0:T(1,128)S(1)}, f32[4,5,1,128]{3,2,1,0:T(1,128)S(1)}, u32[]{:S(2)}, u32[]{:S(2)}) collective-permute-start(f32[4,5,1,128]{3,2,1,0:T(1,128)S(1)} %get-tuple-element.386), channel_id=1, source_target_pairs={{8,0},{16,8},{24,16},{32,24},{40,32},{48,40},{56,48},{64,56},{72,6... | collective-permute-start | bytes 30728 | tf_op jit(solution)/shard_map/ppermute | solution.py:34
  264.6 95.7 %reduce-scatter.33.cloned.1.call-start = ((), (), s32[]{:S(2)}) async-start(), calls=%async_computation.12 | async-start | bytes 589824
  265.7 28.5 %copy-start.25 = (f32[4,4,128]{0,2,1:T(8,128)S(1)}, f32[4,4,128]{0,2,1:T(8,128)}, u32[]{:S(2)}) copy-start(f32[4,4,128]{0,2,1:T(8,128)} %copy-done.24) | copy-start | bytes 24580
  265.7 28.5 %copy-start.27 = (f32[4,4,128]{0,2,1:T(8,128)S(1)}, f32[4,4,128]{0,2,1:T(8,128)}, u32[]{:S(2)}) copy-start(f32[4,4,128]{0,2,1:T(8,128)} %copy-done.26) | copy-start | bytes 24580
  298.0 7.5 collective-permute-start.8
  301.6 25.3 %collective-permute-start.9 = (f32[4,5,1,128]{3,2,1,0:T(1,128)S(1)}, f32[4,5,1,128]{3,2,1,0:T(1,128)S(1)}, u32[]{:S(2)}, u32[]{:S(2)}) collective-permute-start(f32[4,5,1,128]{3,2,1,0:T(1,128)S(1)} %get-tuple-element.384), channel_id=1, source_target_pairs={{8,0},{16,8},{24,16},{32,24},{40,32},{48,40},{56,48},{64,56},{72,6... | collective-permute-start | bytes 30728 | tf_op jit(solution)/shard_map/ppermute | solution.py:34
  331.8 95.7 %reduce-scatter.35.cloned.1.call-start = ((), (), s32[]{:S(2)}) async-start(), calls=%async_computation.13 | async-start | bytes 589824
  333.1 28.3 %copy-start.29 = (f32[4,4,128]{0,2,1:T(8,128)S(1)}, f32[4,4,128]{0,2,1:T(8,128)}, u32[]{:S(2)}) copy-start(f32[4,4,128]{0,2,1:T(8,128)} %copy-done.28) | copy-start | bytes 24580
  333.1 28.3 %copy-start.31 = (f32[4,4,128]{0,2,1:T(8,128)S(1)}, f32[4,4,128]{0,2,1:T(8,128)}, u32[]{:S(2)}) copy-start(f32[4,4,128]{0,2,1:T(8,128)} %copy-done.30) | copy-start | bytes 24580
  365.3 7.5 collective-permute-start.10
  368.8 25.3 %collective-permute-start.11 = (f32[4,5,1,128]{3,2,1,0:T(1,128)S(1)}, f32[4,5,1,128]{3,2,1,0:T(1,128)S(1)}, u32[]{:S(2)}, u32[]{:S(2)}) collective-permute-start(f32[4,5,1,128]{3,2,1,0:T(1,128)S(1)} %get-tuple-element.382), channel_id=1, source_target_pairs={{8,0},{16,8},{24,16},{32,24},{40,32},{48,40},{56,48},{64,56},{72,6... | collective-permute-start | bytes 30728 | tf_op jit(solution)/shard_map/ppermute | solution.py:34
  399.1 95.9 %reduce-scatter.37.cloned.1.call-start = ((), (), s32[]{:S(2)}) async-start(), calls=%async_computation.14 | async-start | bytes 589824
  400.1 28.5 %copy-start.33 = (f32[4,4,128]{0,2,1:T(8,128)S(1)}, f32[4,4,128]{0,2,1:T(8,128)}, u32[]{:S(2)}) copy-start(f32[4,4,128]{0,2,1:T(8,128)} %copy-done.32) | copy-start | bytes 24580
  400.2 28.5 %copy-start.35 = (f32[4,4,128]{0,2,1:T(8,128)S(1)}, f32[4,4,128]{0,2,1:T(8,128)}, u32[]{:S(2)}) copy-start(f32[4,4,128]{0,2,1:T(8,128)} %copy-done.34) | copy-start | bytes 24580
  432.5 7.5 collective-permute-start.12
  436.0 25.5 %collective-permute-start.13 = (f32[4,5,1,128]{3,2,1,0:T(1,128)S(1)}, f32[4,5,1,128]{3,2,1,0:T(1,128)S(1)}, u32[]{:S(2)}, u32[]{:S(2)}) collective-permute-start(f32[4,5,1,128]{3,2,1,0:T(1,128)S(1)} %get-tuple-element.380), channel_id=1, source_target_pairs={{8,0},{16,8},{24,16},{32,24},{40,32},{48,40},{56,48},{64,56},{72,6... | collective-permute-start | bytes 30728 | tf_op jit(solution)/shard_map/ppermute | solution.py:34
  466.5 96.0 %reduce-scatter.39.cloned.1.call-start = ((), (), s32[]{:S(2)}) async-start(), calls=%async_computation.15 | async-start | bytes 589824
  467.6 28.5 %copy-start.37 = (f32[4,4,128]{0,2,1:T(8,128)S(1)}, f32[4,4,128]{0,2,1:T(8,128)}, u32[]{:S(2)}) copy-start(f32[4,4,128]{0,2,1:T(8,128)} %copy-done.36) | copy-start | bytes 24580
  467.6 28.5 %copy-start.39 = (f32[4,4,128]{0,2,1:T(8,128)S(1)}, f32[4,4,128]{0,2,1:T(8,128)}, u32[]{:S(2)}) copy-start(f32[4,4,128]{0,2,1:T(8,128)} %copy-done.38) | copy-start | bytes 24580
  500.0 7.5 collective-permute-start.14
  503.5 25.3 %collective-permute-start.15 = (f32[4,5,1,128]{3,2,1,0:T(1,128)S(1)}, f32[4,5,1,128]{3,2,1,0:T(1,128)S(1)}, u32[]{:S(2)}, u32[]{:S(2)}) collective-permute-start(f32[4,5,1,128]{3,2,1,0:T(1,128)S(1)} %get-tuple-element.378), channel_id=1, source_target_pairs={{8,0},{16,8},{24,16},{32,24},{40,32},{48,40},{56,48},{64,56},{72,6... | collective-permute-start | bytes 30728 | tf_op jit(solution)/shard_map/ppermute | solution.py:34
  535.1 28.5 %copy-start.16 = (f32[4,4,128]{0,2,1:T(8,128)S(1)}, f32[4,4,128]{0,2,1:T(8,128)}, u32[]{:S(2)}) copy-start(f32[4,4,128]{0,2,1:T(8,128)} %copy-done.15) | copy-start | bytes 24580
  535.1 28.5 %copy-start.18 = (f32[4,4,128]{0,2,1:T(8,128)S(1)}, f32[4,4,128]{0,2,1:T(8,128)}, u32[]{:S(2)}) copy-start(f32[4,4,128]{0,2,1:T(8,128)} %copy-done.17) | copy-start | bytes 24580
  569.4 27.1 %copy-start.44 = (f32[2,128]{1,0:T(2,128)S(1)}, f32[2,128]{1,0:T(2,128)}, u32[]{:S(2)}) copy-start(f32[2,128]{1,0:T(2,128)} %copy-done.42) | copy-start | bytes 3076
  569.8 50.2 %copy-start.45 = (f32[2,128]{1,0:T(2,128)S(1)}, f32[2,128]{1,0:T(2,128)}, u32[]{:S(2)}) copy-start(f32[2,128]{1,0:T(2,128)} %copy-done.42) | copy-start | bytes 3076
  569.9 72.2 %copy-start.46 = (f32[2,128]{1,0:T(2,128)S(1)}, f32[2,128]{1,0:T(2,128)}, u32[]{:S(2)}) copy-start(f32[2,128]{1,0:T(2,128)} %copy-done.42) | copy-start | bytes 3076
  570.2 95.3 %copy-start.47 = (f32[2,128]{1,0:T(2,128)S(1)}, f32[2,128]{1,0:T(2,128)}, u32[]{:S(2)}) copy-start(f32[2,128]{1,0:T(2,128)} %copy-done.42) | copy-start | bytes 3076
  570.5 117.2 %copy-start.48 = (f32[2,128]{1,0:T(2,128)S(1)}, f32[2,128]{1,0:T(2,128)}, u32[]{:S(2)}) copy-start(f32[2,128]{1,0:T(2,128)} %copy-done.42) | copy-start | bytes 3076
  570.6 140.5 %copy-start.49 = (f32[2,128]{1,0:T(2,128)S(1)}, f32[2,128]{1,0:T(2,128)}, u32[]{:S(2)}) copy-start(f32[2,128]{1,0:T(2,128)} %copy-done.42) | copy-start | bytes 3076
  571.0 162.3 %copy-start.50 = (f32[2,128]{1,0:T(2,128)S(1)}, f32[2,128]{1,0:T(2,128)}, u32[]{:S(2)}) copy-start(f32[2,128]{1,0:T(2,128)} %copy-done.42) | copy-start | bytes 3076
  571.1 185.6 %copy-start.43 = (f32[2,128]{1,0:T(2,128)S(1)}, f32[2,128]{1,0:T(2,128)}, u32[]{:S(2)}) copy-start(f32[2,128]{1,0:T(2,128)} %copy-done.42) | copy-start | bytes 3076
  (60 other events, 603.3 us)
Sparse Core Ops, SparseCore 0:
  58.1 28.4 reduce-scatter.24
  126.0 28.2 reduce-scatter.26
  196.0 28.2 reduce-scatter.28
  264.7 28.3 reduce-scatter.30
  331.9 28.2 reduce-scatter.32
  399.2 28.3 reduce-scatter.34
  466.6 28.2 reduce-scatter.36
  534.2 28.3 reduce-scatter.38
where the time goes:
time: 775 us; the launch traced here: 765 us
  blocking collectives  276 us (36%)
  waiting for transfers between devices  208 us (27%)
  local copies, waits for them, and re-layouts  156 us (20%)
  other arithmetic  61.7 us (8%)
  starting transfers between devices  44.3 us (6%)
  between operations  18.2 us (2%)
    unnamed x16, waiting for transfers between devices  207 us
    all_gather x8, blocking collectives, carried_in(): gathered = lax.all_gather(part, axis)  183 us
    all_gather x8, blocking collectives, on_device(): lax.all_gather(jnp.stack([part_a, part_b]), 'lc', axis=3, tiled=True)  92.6 us
    unnamed x213, local copies, waits for them, and re-layouts  36 us
    ppermute x8, starting transfers between devices, with_halo(): lax.ppermute(lax.slice_in_dim(block, 0, width, axis=dim), axis, backward)  31.4 us
    mul x8, other arithmetic, cell_terms(): pce_demand = totals * speeds  22 us
    gather x16, local copies, waits for them, and re-layouts, on_device(): take_a = jnp.take(end_pack[0], feed_a, axis=2)  19.9 us
    gather x16, local copies, waits for them, and re-layouts, on_device(): take_b = jnp.take(end_pack[1], feed_b, axis=2)  19.8 us
  transfers between devices with their start and end apart: 24, of which 11 were waited for; matrix products, arithmetic and copies ran while one was open for 14% of the time, Pallas kernels for 0%

commit v1 on v0

v1 whole, which is shorter than its diff:
```python
import jax
import jax.numpy as jnp
from jax import lax
from jax.experimental import pallas as pl
from jax.experimental.pallas import tpu as pltpu
from jax.sharding import PartitionSpec as P

STEPS = 8
LANES = 4
CLASSES = 3
ROWS = 16
WIDTH = 128
CELLS_HERE = 128
BIG = 1e30
F32 = jnp.float32
RAMP_UNIT = 0.01
RAMP_FRACTION = (0.56, 0.16, 0.08)
VMEM_BYTES = 40 * 1024 * 1024

HEAD_DEPTH = 27
TAIL_DEPTH = 35
RAMP_ROW = 108
FEED_ROW = 140
SHARE_ROW = 141
INVERSE_ROW = 142
RECORD = 152


def inverse(x):
    r = pl.reciprocal(x, approx=True)
    return r * (2.0 - x * r)


def total_of(state):
    return state[0] + 1.5 * state[1] + 2.5 * state[2]


def supply_of(totals, cap, jam, wave):
    return jnp.maximum(jnp.minimum(cap, wave * (jam - totals)), 0.0)


def sent_share(totals, cap, next_supply):
    return jnp.minimum(0.5, jnp.minimum(cap, next_supply) * inverse(totals))


def pick(code, table, count):
    values = [table[i] for i in range(count)]
    bit = 1
    while len(values) > 1:
        on = (code & bit) != 0
        values = [jnp.where(on, values[i + 1], values[i]) for i in range(0, len(values), 2)]
        bit *= 2
    return values[0]


def wave_of(cap, jam):
    return cap / (jam - 2.0 * cap)


def lane_change(state, adjacent, coef):
    moving = [
        [(adjacent[p] * coef[k]) * (state[p][k] - state[p + 1][k]) for k in range(CLASSES)]
        for p in range(LANES - 1)
    ]
    out = []
    for lane in range(LANES):
        row = []
        for k in range(CLASSES):
            value = state[lane][k]
            if lane < LANES - 1:
                value = value - moving[lane][k]
            if lane > 0:
                value = value + moving[lane - 1][k]
            row.append(value)
        out.append(row)
    return out


def middle(a, b, c):
    return jnp.maximum(jnp.minimum(a, b), jnp.minimum(jnp.maximum(a, b), c))


def window(count, refs, step, coef, inject, mask, scan):
    st, tot, cap, jam, wave, adj, level, acc, low = refs
    last = count - 1

    def supply(v):
        return [
            supply_of(tot[lane, v], cap[lane, v], jam[lane, v], wave[lane, v])
            for lane in range(LANES)
        ]

    def flux(v, next_supply):
        out = []
        for lane in range(LANES):
            share = sent_share(tot[lane, v], cap[lane, v], next_supply[lane])
            out.append([st[lane * CLASSES + k, v] * share for k in range(CLASSES)])
        return out

    wrapped = [pltpu.roll(x, 7, 0) for x in supply(0)]
    final = flux(last, wrapped)
    before = [[pltpu.roll(x, 1, 0) for x in row] for row in final]
    running = lowest = None
    for v in range(count):
        leaving = flux(v, supply(v + 1)) if v < last else final
        came, gone = inject(v, before, leaving)
        state = [
            [(st[lane * CLASSES + k, v] + came[lane][k]) - gone[lane][k] for k in range(CLASSES)]
            for lane in range(LANES)
        ]
        state = lane_change(state, [adj[p, v] for p in range(LANES - 1)], coef)
        sums = []
        for lane in range(LANES):
            for k in range(CLASSES):
                st[lane * CLASSES + k, v] = state[lane][k]
            sums.append(total_of(state[lane]))
            tot[lane, v] = sums[lane]
        excess = 0.25 * ((sums[0] + sums[1]) + (sums[2] + sums[3])) - level[v]
        excess = jnp.where(mask(v), excess, 0.0)
        running = excess if running is None else running + excess
        lowest = running if lowest is None else jnp.minimum(lowest, running)
        acc[1, v] = running
        low[step, v] = lowest
        before = leaving
    carry, floor = scan(running, lowest)
    for v in range(count):
        acc[0, v] = acc[0, v] + (carry + acc[1, v])
        low[step, v] = jnp.minimum(floor, carry + low[step, v])


def fill(count, stride, refs, density, cap_code, jam_code, adjacency, cap_table, jam_table):
    st, tot, cap, jam, wave, adj, level, acc = refs
    for v in range(count):
        rows = pl.ds(v, 8, stride=stride)
        around = None
        for lane in range(LANES):
            state = [density(lane * CLASSES + k, rows) for k in range(CLASSES)]
            for k in range(CLASSES):
                st[lane * CLASSES + k, v] = state[k]
            tot[lane, v] = total_of(state)
            c = pick(cap_code(lane, rows), cap_table, 8)
            j = pick(jam_code(lane, rows), jam_table, 4)
            cap[lane, v] = c
            jam[lane, v] = j
            wave[lane, v] = wave_of(c, j)
            around = c if around is None else around + c
        for p in range(LANES - 1):
            adj[p, v] = adjacency(p, rows)
        level[v] = 0.5 * around
        acc[0, v] = jnp.zeros((8, WIDTH), F32)


def pack_kernel(
    cap_table, jam_table, coef_ref, feed_a, feed_b, feed_a_row, feed_b_row, share_row, prio_row,
    ramp, d_lo, d_hi, c_lo, c_hi, j_lo, j_hi, a_lo, a_hi, fwd, bwd, zone,
):
    tail = lax.axis_index("corr") == ROWS - 1
    place = lax.axis_index("lc")
    for out, d, c, j, a in ((bwd, d_lo, c_lo, j_lo, a_lo), (fwd, d_hi, c_hi, j_hi, a_hi)):
        row = 0
        for ref, n in ((d, 12), (c, 4), (j, 4), (a, 3)):
            for i in range(n):
                out[pl.ds(row * 8, 8), :] = ref[i].astype(F32)
                row += 1
    coef = [coef_ref[k] for k in range(CLASSES)]

    def own(lo, hi, i):
        return jnp.where(tail, hi[i], lo[i])

    cap_code = [own(c_lo, c_hi, i) for i in range(LANES)]
    jam_code = [own(j_lo, j_hi, i) for i in range(LANES)]
    near = [own(a_lo, a_hi, i).astype(F32) for i in range(LANES - 1)]
    cap = [pick(x, cap_table, 8) for x in cap_code]
    jam = [pick(x, jam_table, 4) for x in jam_code]
    wave = [wave_of(c, j) for c, j in zip(cap, jam)]
    state = [[own(d_lo, d_hi, lane * CLASSES + k) for k in range(CLASSES)] for lane in range(LANES)]
    history = []
    for d in range(4):
        totals = [total_of(x) for x in state]
        supply = [supply_of(totals[i], cap[i], jam[i], wave[i]) for i in range(LANES)]
        ahead = [pltpu.roll(x, 7, 0) for x in supply]
        out = []
        for i in range(LANES):
            share = sent_share(totals[i], cap[i], ahead[i])
            out.append([x * share for x in state[i]])
        came = [[pltpu.roll(x, 1, 0) for x in row] for row in out]
        history.append((state, ahead, came))
        if d < 3:
            state = [
                [(state[i][k] + came[i][k]) - out[i][k] for k in range(CLASSES)]
                for i in range(LANES)
            ]
            state = lane_change(state, near, coef)
    codes = [x.astype(F32) for x in cap_code + jam_code] + near

    def put(row, value, at):
        zone[pl.ds(row, 1), :] = value[at : at + 1, :]

    @pl.when(tail)
    def _():
        for d in range(4):
            state, _, came = history[d]
            for i in range(LANES):
                for k in range(CLASSES):
                    put(TAIL_DEPTH * d + i * CLASSES + k, state[i][k], 7 - d)
                    put(TAIL_DEPTH * d + 12 + i * CLASSES + k, came[i][k], 7 - d)
            for n, x in enumerate(codes):
                put(TAIL_DEPTH * d + 24 + n, x, 7 - d)
        zone[pl.ds(FEED_ROW, 1), :] = feed_b_row[...].astype(F32)
        zone[pl.ds(SHARE_ROW, 1), :] = share_row[...]

    @pl.when(jnp.logical_not(tail))
    def _():
        for d in range(4):
            state, ahead, _ = history[d]
            for i in range(LANES):
                for k in range(CLASSES):
                    put(HEAD_DEPTH * d + i * CLASSES + k, state[i][k], d)
                put(HEAD_DEPTH * d + 12 + i, ahead[i], d)
            for n, x in enumerate(codes):
                put(HEAD_DEPTH * d + 16 + n, x, d)
        zone[pl.ds(RAMP_ROW, 32), :] = ramp[...].astype(F32)
        zone[pl.ds(FEED_ROW, 1), :] = feed_a_row[...].astype(F32)
        zone[pl.ds(SHARE_ROW, 1), :] = prio_row[...]

    index = lax.broadcasted_iota(jnp.int32, (8, WIDTH), 0) * WIDTH + lax.broadcasted_iota(
        jnp.int32, (8, WIDTH), 1
    )

    def note(c, found):
        feed = jnp.where(tail, feed_b[c], feed_a[c])
        return jnp.where(index == feed, place * WIDTH + c, found)

    found = lax.fori_loop(0, WIDTH, note, jnp.zeros((8, WIDTH), jnp.int32), unroll=16)
    zone[pl.ds(INVERSE_ROW, 8), :] = found.astype(F32)
    zone[pl.ds(INVERSE_ROW + 8, 2), :] = jnp.zeros((2, WIDTH), F32)


def inner_kernel(
    cap_table, jam_table, coef_ref, density, cap_code, jam_code, adjacency,
    traffic, acc_out, low, stats, st, tot, cap, jam, wave, adj, level, acc,
):
    coef = [coef_ref[k] for k in range(CLASSES)]
    fill(
        16, 16, (st, tot, cap, jam, wave, adj, level, acc),
        lambda i, rows: density[i, rows, :],
        lambda i, rows: cap_code[i, rows, :],
        lambda i, rows: jam_code[i, rows, :],
        lambda i, rows: adjacency[i, rows, :].astype(F32),
        cap_table, jam_table,
    )
    sub = lax.broadcasted_iota(jnp.int32, (8, WIDTH), 0)

    def one(step, carry):
        def scan(running, lowest):
            total, least = running, lowest
            for shift in (1, 2, 4):
                here = sub >= shift
                t = jnp.where(here, pltpu.roll(total, shift, 0), 0.0)
                m = jnp.where(here, pltpu.roll(least, shift, 0), BIG)
                least = jnp.minimum(m, t + least)
                total = t + total
            stats[0, pl.ds(step, 1), :] = total[7:8, :]
            stats[1, pl.ds(step, 1), :] = least[7:8, :]
            return (
                jnp.where(sub >= 1, pltpu.roll(total, 1, 0), 0.0),
                jnp.where(sub >= 1, pltpu.roll(least, 1, 0), BIG),
            )

        window(
            16, (st, tot, cap, jam, wave, adj, level, acc, low), step, coef,
            lambda v, before, leaving: (before, leaving),
            lambda v: (sub != 0) if v < 8 else (sub != 7),
            scan,
        )
        return carry

    lax.fori_loop(0, STEPS, one, 0)
    for v in range(16):
        for i in range(LANES * CLASSES):
            traffic[i, pl.ds(v, 8, stride=16), :] = st[i, v]
        acc_out[v] = acc[0, v]


def junctions(near_here, zone, inj, spare_rows, cap_table, jam_table, coef):
    head_row = lax.axis_index("corr") == 0

    def head(row):
        return zone[pl.ds(row * 8, 8), :]

    def tail(row):
        return zone[pl.ds((RECORD + row) * 8, 8), :]

    def whole(x):
        return x.astype(jnp.int32)

    feed_a = whole(head(FEED_ROW))
    feed_b = whole(tail(FEED_ROW))
    prio = head(SHARE_ROW)
    share = tail(SHARE_ROW)
    for side, read in enumerate((head, tail)):
        for i in range(8):
            spare_rows[pl.ds(side * 8 + i, 1), :] = jnp.sum(
                read(INVERSE_ROW + i), axis=0, keepdims=True
            )
    back_from_a = whole(spare_rows[pl.ds(0, 8), :])
    back_from_b = whole(spare_rows[pl.ds(8, 8), :])

    def plan(index):
        chunk = index // WIDTH
        lane = index - chunk * WIDTH
        return lane, [chunk == i for i in range(1, 8)]

    plan_a, plan_b, plan_ra, plan_rb = (
        plan(x) for x in (feed_a, feed_b, back_from_a, back_from_b)
    )

    def permute(x, how):
        lane, masks = how
        out = None
        for i in range(8):
            row = jnp.broadcast_to(x[i : i + 1, :], (8, WIDTH))
            got = jnp.take_along_axis(row, lane, axis=1, mode="promise_in_bounds")
            out = got if out is None else jnp.where(masks[i - 1], got, out)
        return out

    def statics(read, base):
        cap = [pick(whole(read(base + i)), cap_table, 8) for i in range(LANES)]
        jam = [pick(whole(read(base + 4 + i)), jam_table, 4) for i in range(LANES)]
        wave = [wave_of(c, j) for c, j in zip(cap, jam)]
        return cap, jam, wave, [read(base + 8 + p) for p in range(LANES - 1)]

    head_fixed = [statics(head, HEAD_DEPTH * d + 16) for d in range(4)]
    tail_fixed = [statics(tail, TAIL_DEPTH * d + 24) for d in range(4)]

    def first(read, base):
        return [[read(base + i * CLASSES + k) for k in range(CLASSES)] for i in range(LANES)]

    def supplies(state, fixed):
        return [
            supply_of(total_of(state[i]), fixed[0][i], fixed[1][i], fixed[2][i])
            for i in range(LANES)
        ]

    def fluxes(state, fixed, next_supply):
        out = []
        for i in range(LANES):
            q = sent_share(total_of(state[i]), fixed[0][i], next_supply[i])
            out.append([x * q for x in state[i]])
        return out

    heads, tails = {}, {}
    for step in range(STEPS):
        if step < 4:
            heads[step] = first(head, HEAD_DEPTH * step)
            tails[step] = first(tail, TAIL_DEPTH * step)
        deep = min(step, 6 - step)
        supply = supplies(heads[0], head_fixed[0])
        arriving, rates = [], []
        for i in range(LANES):
            state = tails[0][i]
            speed = jnp.minimum(0.5, tail_fixed[0][0][i] * inverse(total_of(state)))
            demand = [x * speed for x in state]
            part_a = [share * x for x in demand]
            part_b = [x - y for x, y in zip(demand, part_a)]
            take_a = [permute(x, plan_a) for x in part_a]
            take_b = [permute(x, plan_b) for x in part_b]
            need_a = total_of(take_a)
            need_b = total_of(take_b)
            s = supply[i]
            share_a = prio * s
            share_b = (1.0 - prio) * s
            pass_a = jnp.minimum(need_a, middle(need_a, s - need_b, share_a))
            pass_b = jnp.minimum(need_b, middle(need_b, s - need_a, share_b))
            rate_a = pass_a / need_a
            rate_b = pass_b / need_b
            ramp = jnp.minimum(
                head(RAMP_ROW + step * LANES + i) * RAMP_UNIT,
                jnp.maximum((s - pass_a) - pass_b, 0.0),
            )
            arriving.append(
                [
                    (take_a[k] * rate_a + take_b[k] * rate_b) + RAMP_FRACTION[k] * ramp
                    for k in range(CLASSES)
                ]
            )
            back_a = permute(rate_a, plan_ra)
            back_b = permute(rate_b, plan_rb)
            rates.append([part_a[k] * back_a + part_b[k] * back_b for k in range(CLASSES)])
        for i in range(LANES):
            for k in range(CLASSES):
                inj[pl.ds((step * 12 + i * CLASSES + k) * 8, 8), :] = jnp.where(
                    head_row, arriving[i][k], rates[i][k]
                )
        if step == STEPS - 1:
            break
        new_heads, new_tails = {}, {}
        came, gone = arriving, rates
        for d in range(deep + 1):
            if d < deep or deep < step:
                ahead = supplies(heads[d + 1], head_fixed[d + 1])
                entering = fluxes(tails[d + 1], tail_fixed[d + 1], supplies(tails[d], tail_fixed[d]))
            else:
                ahead = [head(HEAD_DEPTH * d + 12 + i) for i in range(LANES)]
                entering = first(tail, TAIL_DEPTH * d + 12)
            out = fluxes(heads[d], head_fixed[d], ahead)
            moved = [
                [(heads[d][i][k] + came[i][k]) - out[i][k] for k in range(CLASSES)]
                for i in range(LANES)
            ]
            new_heads[d] = lane_change(moved, head_fixed[d][3], coef)
            moved = [
                [(tails[d][i][k] + entering[i][k]) - gone[i][k] for k in range(CLASSES)]
                for i in range(LANES)
            ]
            new_tails[d] = lane_change(moved, tail_fixed[d][3], coef)
            came, gone = out, entering
        heads, tails = new_heads, new_tails


def edge_kernel(
    cap_table, jam_table, coef_ref, d_lo, d_hi, c_lo, c_hi, j_lo, j_hi, a_lo, a_hi, left, right,
    ends_here, ends_other, inner, traffic_in, traffic, segment, aux, acc_out, low,
    nat, zone, inj, spare_rows, st, tot, cap, jam, wave, adj, level, acc, out, sem,
):
    del traffic_in
    row = lax.axis_index("corr")
    place = lax.axis_index("lc")
    coef = [coef_ref[k] for k in range(CLASSES)]
    first_row = row == 0
    last_row = row == ROWS - 1

    @pl.when(jnp.logical_or(first_row, last_row))
    def _():
        for swap, ends in ((0, ends_here), (1, ends_other)):
            core = jnp.where(swap == 0, place % 2, 1 - place % 2)
            for z in range(4):
                for m in range(2):
                    side = jnp.where(first_row, m, 1 - m)
                    base = side * (RECORD * 8) + 2 * z + core
                    for r in range(RECORD // 8):
                        zone[pl.ds(base + r * 64, 8, stride=8), :] = ends[
                            z, pl.ds(m * RECORD + r * 8, 8), :
                        ]
        junctions(place, zone, inj, spare_rows, cap_table, jam_table, coef)

    index = 0
    for n, lo, hi in ((12, d_lo, d_hi), (4, c_lo, c_hi), (4, j_lo, j_hi), (3, a_lo, a_hi)):
        for i in range(n):
            base = index * 48
            nat[pl.ds(base, 8), :] = left[pl.ds(index * 8, 8), :]
            nat[pl.ds(base + 8, 16), :] = lo[i].astype(F32)
            nat[pl.ds(base + 24, 16), :] = hi[i].astype(F32)
            nat[pl.ds(base + 40, 8), :] = right[pl.ds(index * 8, 8), :]
            index += 1

    def rows_of(base):
        def read(i, rows):
            return nat[pl.ds((base + i) * 48 + rows.start, 8, stride=6), :]

        return read

    def code_of(base):
        read = rows_of(base)
        return lambda i, rows: read(i, rows).astype(jnp.int32)

    fill(
        6, 6, (st, tot, cap, jam, wave, adj, level, acc),
        rows_of(0), code_of(12), code_of(16), rows_of(20), cap_table, jam_table,
    )
    sub = lax.broadcasted_iota(jnp.int32, (8, WIDTH), 0)
    in_strip = sub % 4
    at_head = jnp.logical_and(sub == 1, first_row)
    at_tail = jnp.logical_and(sub == 6, last_row)

    def one(step, carry):
        def injected(i, k):
            return jnp.broadcast_to(
                inj[pl.ds((step * 12 + i * CLASSES + k) * 8 + place, 1), :], (8, WIDTH)
            )

        def inject(v, before, leaving):
            came, gone = before, leaving
            if v == 2:
                came = [
                    [jnp.where(at_head, injected(i, k), before[i][k]) for k in range(CLASSES)]
                    for i in range(LANES)
                ]
            if v == 3:
                gone = [
                    [jnp.where(at_tail, injected(i, k), leaving[i][k]) for k in range(CLASSES)]
                    for i in range(LANES)
                ]
            return came, gone

        def mask(v):
            if v < 2:
                return in_strip == 2
            if v < 4:
                return jnp.logical_or(in_strip == 1, in_strip == 2)
            return in_strip == 1

        def scan(running, lowest):
            second = in_strip == 2
            carry = jnp.where(second, pltpu.roll(running, 1, 0), 0.0)
            floor = jnp.where(second, pltpu.roll(lowest, 1, 0), BIG)
            total = carry + running
            least = jnp.minimum(floor, carry + lowest)
            aux[0, pl.ds(step, 1), :] = total[2:3, :]
            aux[1, pl.ds(step, 1), :] = least[2:3, :]
            aux[2, pl.ds(step, 1), :] = total[6:7, :]
            aux[3, pl.ds(step, 1), :] = least[6:7, :]
            return carry, floor

        window(
            6, (st, tot, cap, jam, wave, adj, level, acc, low), step, coef, inject, mask, scan
        )
        return carry

    lax.fori_loop(0, STEPS, one, 0)
    for v in range(6):
        for i in range(LANES * CLASSES):
            nat[pl.ds(i * 48 + v, 8, stride=6), :] = st[i, v]
        acc_out[v] = acc[0, v]
    for i in range(LANES * CLASSES):
        out[0, i] = nat[pl.ds(i * 48 + 8, 8), :]
        out[1, i] = nat[pl.ds(i * 48 + 32, 8), :]
    copies = [
        pltpu.make_async_copy(out.at[0], traffic.at[:, pl.ds(0, 8), :], sem.at[0]),
        pltpu.make_async_copy(out.at[1], traffic.at[:, pl.ds(CELLS_HERE - 8, 8), :], sem.at[1]),
    ]
    for copy in copies:
        copy.start()
    left_sum, left_low = aux[0], aux[1]
    most_sum = left_sum + inner[0]
    most_low = jnp.minimum(left_low, left_sum + inner[1])
    all_sum = most_sum + aux[2]
    all_low = jnp.minimum(most_low, most_sum + aux[3])
    for i in range(ROWS):
        segment[i, 0] = all_sum
        segment[i, 1] = all_low
    for copy in copies:
        copy.wait()


def count_kernel(
    segments, aux, inner, acc, low, edge_acc, edge_low, queue, sums, floors, nat
):
    row = lax.axis_index("corr")
    total = jnp.zeros((8, WIDTH), F32)
    least = jnp.zeros((8, WIDTH), F32)
    for i in range(ROWS - 1):
        on = i < row
        least = jnp.where(on, jnp.minimum(least, total + segments[i, 1]), least)
        total = jnp.where(on, total + segments[i, 0], total)
    mid_total = total + aux[0]
    mid_least = jnp.minimum(least, total + aux[1])
    end_total = mid_total + inner[0]
    end_least = jnp.minimum(mid_least, mid_total + inner[1])
    for n, (t, m) in enumerate(((total, least), (mid_total, mid_least), (end_total, end_least))):
        sums[n] = t
        floors[n] = m
    scale = 1.0 / (STEPS * CELLS_HERE * ROWS)
    left = lax.broadcasted_iota(jnp.int32, (8, WIDTH), 0) < 4

    def spread(ref, n, step):
        return jnp.broadcast_to(ref[n, pl.ds(step, 1), :], (8, WIDTH))

    inside = [(spread(sums, 1, s), spread(floors, 1, s)) for s in range(STEPS)]
    for v in range(16):
        value = acc[v]
        for s in range(STEPS):
            value = value + (inside[s][0] - jnp.minimum(inside[s][1], inside[s][0] + low[s, v]))
        queue[pl.ds(v, 8, stride=16), :] = value * scale
    edges = [
        (
            jnp.where(left, spread(sums, 0, s), spread(sums, 2, s)),
            jnp.where(left, spread(floors, 0, s), spread(floors, 2, s)),
        )
        for s in range(STEPS)
    ]
    for v in range(6):
        value = edge_acc[v]
        for s in range(STEPS):
            value = value + (edges[s][0] - jnp.minimum(edges[s][1], edges[s][0] + edge_low[s, v]))
        nat[pl.ds(v, 8, stride=6), :] = value * scale
    queue[pl.ds(0, 8), :] = nat[pl.ds(8, 8), :]
    queue[pl.ds(CELLS_HERE - 8, 8), :] = nat[pl.ds(32, 8), :]


def shape(*dims):
    return jax.ShapeDtypeStruct(dims, F32)


def full(*dims):
    return pl.BlockSpec(dims, lambda i: (0,) * len(dims))


def part(place, *dims):
    return pl.BlockSpec(dims, lambda i: (0, place, 0))


SCALARS = pl.BlockSpec(memory_space=pltpu.SMEM)


def call(kernel, name, args, in_specs, outs, out_specs, scratch=(), aliases=None, flops=0):
    return pl.pallas_call(
        kernel,
        grid=(1,),
        in_specs=in_specs,
        out_specs=out_specs,
        out_shape=outs,
        scratch_shapes=scratch,
        input_output_aliases=aliases or {},
        compiler_params=pltpu.CompilerParams(vmem_limit_bytes=VMEM_BYTES),
        cost_estimate=pl.CostEstimate(flops=flops, bytes_accessed=4 << 20, transcendentals=0),
        name=name,
    )(*args)


def cells_scratch(count):
    def hold(n):
        return pltpu.VMEM((n, count, 8, WIDTH), F32)

    return [hold(12), hold(4), hold(4), hold(4), hold(4), hold(3), pltpu.VMEM((count, 8, WIDTH), F32), hold(2)]


def on_device(
    density, cap_code, jam_code, adjacency, ramp_code, feed_a, feed_b, turn_share, priority,
    cap_table, jam_table, change_coef,
):
    density = density.reshape(12, CELLS_HERE, WIDTH)
    tables = [cap_table, jam_table, change_coef]
    grids = [density, cap_code, jam_code, adjacency]
    sizes = (12, 4, 4, 3)

    def ends(depth):
        args, specs = [], []
        for x, n in zip(grids, sizes):
            args += [x, x]
            specs += [part(0, n, depth, WIDTH), part(CELLS_HERE // depth - 1, n, depth, WIDTH)]
        return args, specs

    args, specs = ends(8)
    line = [x.reshape(1, WIDTH) for x in (feed_a, feed_b, turn_share, priority)]
    fwd, bwd, record = call(
        pack_kernel, "pack",
        tables + [feed_a, feed_b] + line + [ramp_code.reshape(32, WIDTH)] + args,
        [SCALARS] * 5 + [full(1, WIDTH)] * 4 + [full(32, WIDTH)] + specs,
        [shape(184, WIDTH), shape(184, WIDTH), shape(RECORD, WIDTH)],
        [full(184, WIDTH), full(184, WIDTH), full(RECORD, WIDTH)],
    )
    other_end = lax.ppermute(record, "corr", [(0, ROWS - 1), (ROWS - 1, 0)])
    left = lax.ppermute(fwd, "corr", [(i, i + 1) for i in range(ROWS - 1)])
    right = lax.ppermute(bwd, "corr", [(i + 1, i) for i in range(ROWS - 1)])
    traffic, acc, low, inner = call(
        inner_kernel, "inner", tables + grids,
        [SCALARS] * 3 + [full(n, CELLS_HERE, WIDTH) for n in sizes],
        [shape(12, CELLS_HERE, WIDTH), shape(16, 8, WIDTH), shape(8, 16, 8, WIDTH), shape(2, 8, WIDTH)],
        [full(12, CELLS_HERE, WIDTH), full(16, 8, WIDTH), full(8, 16, 8, WIDTH), full(2, 8, WIDTH)],
        cells_scratch(16),
        flops=1 << 27,
    )
    both = jnp.concatenate([record, other_end], 0)
    ends_here = lax.all_gather(
        both, "lc", axis_index_groups=[[0, 2, 4, 6], [1, 3, 5, 7]]
    )
    ends_other = lax.ppermute(ends_here, "lc", [(i, i ^ 1) for i in range(8)])
    args, specs = ends(16)
    any_space = pl.BlockSpec(memory_space=pl.ANY)
    traffic, segment, aux, edge_acc, edge_low = call(
        edge_kernel, "edges",
        tables + args + [left, right, ends_here, ends_other, inner, traffic],
        [SCALARS] * 3 + specs + [full(184, WIDTH)] * 2 + [full(4, 2 * RECORD, WIDTH)] * 2
        + [full(2, 8, WIDTH), any_space],
        [shape(12, CELLS_HERE, WIDTH), shape(ROWS, 2, 8, WIDTH), shape(4, 8, WIDTH),
         shape(6, 8, WIDTH), shape(8, 6, 8, WIDTH)],
        [any_space, full(ROWS, 2, 8, WIDTH), full(4, 8, WIDTH), full(6, 8, WIDTH),
         full(8, 6, 8, WIDTH)],
        [pltpu.VMEM((23 * 48, WIDTH), F32), pltpu.VMEM((2 * RECORD * 8, WIDTH), F32),
         pltpu.VMEM((STEPS * 12 * 8, WIDTH), F32), pltpu.VMEM((16, WIDTH), F32)]
        + cells_scratch(6)
        + [pltpu.VMEM((2, 12, 8, WIDTH), F32), pltpu.SemaphoreType.DMA((2,))],
        aliases={16: 0},
    )
    segments = lax.all_to_all(segment, "corr", 0, 0)
    queue = call(
        count_kernel, "count", [segments, aux, inner, acc, low, edge_acc, edge_low],
        [full(ROWS, 2, 8, WIDTH), full(4, 8, WIDTH), full(2, 8, WIDTH), full(16, 8, WIDTH),
         full(8, 16, 8, WIDTH), full(6, 8, WIDTH), full(8, 6, 8, WIDTH)],
        shape(CELLS_HERE, WIDTH), full(CELLS_HERE, WIDTH),
        [pltpu.VMEM((3, 8, WIDTH), F32), pltpu.VMEM((3, 8, WIDTH), F32), pltpu.VMEM((48, WIDTH), F32)],
    )
    return traffic.reshape(LANES, CLASSES, CELLS_HERE, WIDTH), queue


def solution(mesh):
    placed = (
        P(None, None, "corr", "lc"),
        P(None, "corr", "lc"),
        P(None, "corr", "lc"),
        P(None, "corr", "lc"),
        P(None, None, "lc"),
        P("lc"),
        P("lc"),
        P("lc"),
        P("lc"),
        P(),
        P(),
        P(),
    )
    return jax.shard_map(
        on_device,
        mesh=mesh,
        in_specs=placed,
        out_specs=(P(None, None, "corr", "lc"), P("corr", "lc")),
        check_vma=False,
    )
```

time: 775 us -> 67.4 us (0.09); the launches traced: 765 us -> 67 us
  blocking collectives: 276 us -> 32.4 us
  waiting for transfers between devices: 208 us -> 2.41 us
  local copies, waits for them, and re-layouts: 156 us -> 5.39 us
  other arithmetic: 61.7 us -> 0.01 us
  starting transfers between devices: 44.3 us -> 9.91 us
  between operations: 18.2 us -> 0.8 us
  Pallas kernels: 0 us -> 16.1 us
    all_gather x16 -> x1, blocking collectives: 276 us -> 14.6 us  [on_device(): lax.all_gather(both, 'lc', axis_index_groups=[[0, 2, 4, 6], [1, 3, 5, 7]])]
    unnamed x16 -> x0, waiting for transfers between devices: 207 us -> none
    gather x32 -> x0, local copies, waits for them, and re-layouts: 39.7 us -> none  [the longest x16 19.9 us: on_device(): take_a = jnp.take(end_pack[0], feed_a, axis=2)]
    slice x113 -> x0, local copies, waits for them, and re-layouts: 35.4 us -> none  [the longest x6 10.5 us: on_device(): take_b = jnp.take(end_pack[1], feed_b, axis=2)]
    ppermute x16 -> x4, starting transfers between devices: 43.8 us -> 9.91 us  [the longest x1 7.33 us: on_device(): other_end = lax.ppermute(record, 'corr', [(0, ROWS - 1), (ROWS - 1, 0)])]
    unnamed x213 -> x32, local copies, waits for them, and re-layouts: 36 us -> 5.39 us
    mul x64 -> x0, other arithmetic: 27.9 us -> none  [the longest x8 22 us: cell_terms(): pce_demand = totals * speeds]
    scatter x16 -> x0, local copies, waits for them, and re-layouts: 18.2 us -> none  [the longest x8 9.17 us: on_device(): jnp.zeros((lane_count, end_pack.shape[3]), jnp.float32).at[:, feed_a]]
  transfers between devices with their start and end apart: 24 -> 4, of which waited for: 11 -> 1; matrix products, arithmetic and copies ran while one was open for 14% -> 0% of each run, Pallas kernels for 0% -> 9%
where the time goes in v1:
time: 67.4 us; the launch traced here: 67 us
  blocking collectives  32.4 us (48%)
  Pallas kernels  16.1 us (24%)
  starting transfers between devices  9.91 us (15%)
  local copies, waits for them, and re-layouts  5.39 us (8%)
  waiting for transfers between devices  2.41 us (4%)
  between operations  0.8 us (1%)
    all_to_all x1, blocking collectives, on_device(): segments = lax.all_to_all(segment, 'corr', 0, 0)  17.8 us
    pallas_call x4, Pallas kernels, call(): pl.pallas_call(kernel, grid=(1,), in_specs=in_specs, out_specs=out_specs,...  16.1 us
    all_gather x1, blocking collectives, on_device(): lax.all_gather(both, 'lc', axis_index_groups=[[0, 2, 4, 6], [1, 3, 5, 7]])  14.6 us
    ppermute x1, starting transfers between devices, on_device(): other_end = lax.ppermute(record, 'corr', [(0, ROWS - 1), (ROWS - 1, 0)])  7.33 us
    unnamed x32, local copies, waits for them, and re-layouts  5.39 us
    ppermute x1, waiting for transfers between devices, on_device(): other_end = lax.ppermute(record, 'corr', [(0, ROWS - 1), (ROWS - 1, 0)])  2.4 us
  transfers between devices with their start and end apart: 4, of which 1 were waited for; matrix products, arithmetic and copies ran while one was open for 0% of the time, Pallas kernels for 9%

profile of v1, /device:TPU:0, one launch (start us, length us, event | category | flops | bytes accessed | tf_op | source)
XLA Modules:
  0.0 67.0 jit_solution(17964105194355330054)
XLA Ops:
  0.6 0.0 copy-start.12
  0.6 0.0 copy-start.13
  0.7 0.0 copy-start.14
  0.7 0.0 copy-start.15
  0.7 0.0 copy-start.9
  0.7 0.0 copy-start.10
  0.7 0.0 copy-start.11
  0.7 0.6 copy-done.12
  1.3 0.0 copy-done.13
  1.3 0.0 copy-done.14
  1.3 0.0 copy-done.15
  1.3 0.0 copy-done.9
  1.4 0.0 copy-done.10
  1.4 0.0 copy-done.11
  1.4 0.0 copy-start
  1.4 1.1 %copy-done = f32[4,3,128,128]{3,2,1,0:T(8,128)S(1)} copy-done((f32[4,3,128,128]{3,2,1,0:T(8,128)S(1)}, f32[4,3,128,128]{3,2,1,0:T(8,128)}, u32[]{:S(2)}) %copy-start) | copy-done | bytes 786456
  2.5 0.0 copy-start.2
  2.5 0.9 %copy-done.2 = s32[4,128,128]{2,1,0:T(8,128)S(1)} copy-done((s32[4,128,128]{2,1,0:T(8,128)S(1)}, s32[4,128,128]{2,1,0:T(8,128)}, u32[]{:S(2)}) %copy-start.2) | copy-done | bytes 262168
  3.5 0.0 copy-start.4
  3.5 0.9 %copy-done.4 = s32[4,128,128]{2,1,0:T(8,128)S(1)} copy-done((s32[4,128,128]{2,1,0:T(8,128)S(1)}, s32[4,128,128]{2,1,0:T(8,128)}, u32[]{:S(2)}) %copy-start.4) | copy-done | bytes 262168
  4.4 0.0 copy-start.6
  4.4 0.9 %copy-done.6 = s32[3,128,128]{2,1,0:T(8,128)S(1)} copy-done((s32[3,128,128]{2,1,0:T(8,128)S(1)}, s32[3,128,128]{2,1,0:T(8,128)}, u32[]{:S(2)}) %copy-start.6) | copy-done | bytes 196632
  5.3 0.0 copy-start.8
  5.3 0.7 %copy-done.8 = s32[8,4,128]{2,1,0:T(4,128)S(1)} copy-done((s32[8,4,128]{2,1,0:T(4,128)S(1)}, s32[8,4,128]{2,1,0:T(4,128)}, u32[]{:S(2)}) %copy-start.8) | copy-done | bytes 16408
  6.1 0.0 copy-start.5
  6.1 0.0 copy-start.7
  6.1 0.9 %pack.1 = (f32[184,128]{1,0:T(8,128)S(1)}, f32[184,128]{1,0:T(8,128)S(1)}, f32[152,128]{1,0:T(8,128)S(1)}) custom-call(f32[8]{0:T(128)S(1)} %copy-done.9, f32[4]{0:T(128)S(1)} %copy-done.10, f32[3]{0:T(128)S(1)} %copy-done.11, s32[128]{0:T(128)S(1)} %copy-done.12, s32[128]{0:T(128)S(1)} %copy-done.13, s32[1,128]{1,0:T(1,128)S(1)} %bitcast.16, ...), custom_call_target="tpu_custom_call" | custom-call | bytes 4194304 | tf_op jit(solution)/shard_map/pack/pallas_call | solution.py:607
  7.0 0.0 copy-start.1
  7.0 7.3 %collective-permute-start.2 = (f32[152,128]{1,0:T(8,128)S(1)}, f32[152,128]{1,0:T(8,128)S(1)}, u32[]{:S(2)}, u32[]{:S(2)}) collective-permute-start(f32[152,128]{1,0:T(8,128)S(1)} %get-tuple-element.16), channel_id=1, source_target_pairs={{0,120},{120,0},{1,121},{121,1},{2,122},{122,2},{3,123},{123,3},{4... | collective-permute-start | bytes 233480 | tf_op jit(solution)/shard_map/ppermute | solution.py:653
  14.4 2.4 %collective-permute-done.2 = f32[152,128]{1,0:T(8,128)S(1)} collective-permute-done((f32[152,128]{1,0:T(8,128)S(1)}, f32[152,128]{1,0:T(8,128)S(1)}, u32[]{:S(2)}, u32[]{:S(2)}) %collective-permute-start.2) | collective-permute-done | bytes 77856 | tf_op jit(solution)/shard_map/ppermute | solution.py:653
  16.8 0.0 copy-start.3
  16.8 14.6 %all-gather = f32[1216,128]{1,0:T(8,128)S(1)} all-gather(f32[304,128]{1,0:T(8,128)S(1)} %pad_maximum_fusion), channel_id=2, replica_groups={{0,2,4,6},{1,3,5,7},{8,10,12,14},{9,11,13,15},{16,18,20,22},{17,19,21,2..., dimensions={0}, use_global_device_ids=true | all-gather | bytes 778240 | tf_op jit(solution)/shard_map/all_gather | solution.py:665
  31.4 0.0 collective-permute-start.3
  31.4 1.3 %collective-permute-start = (f32[184,128]{1,0:T(8,128)S(1)}, f32[184,128]{1,0:T(8,128)S(1)}, u32[]{:S(2)}, u32[]{:S(2)}) collective-permute-start(f32[184,128]{1,0:T(8,128)S(1)} %get-tuple-element.14), channel_id=1, source_target_pairs={{0,8},{8,16},{16,24},{24,32},{32,40},{40,48},{48,56},{56,64},{64,7... | collective-permute-start | bytes 282632 | tf_op jit(solution)/shard_map/ppermute | solution.py:654
  32.6 1.3 %collective-permute-start.1 = (f32[184,128]{1,0:T(8,128)S(1)}, f32[184,128]{1,0:T(8,128)S(1)}, u32[]{:S(2)}, u32[]{:S(2)}) collective-permute-start(f32[184,128]{1,0:T(8,128)S(1)} %get-tuple-element.15), channel_id=1, source_target_pairs={{8,0},{16,8},{24,16},{32,24},{40,32},{48,40},{56,48},{64,56},{72,6... | collective-permute-start | bytes 282632 | tf_op jit(solution)/shard_map/ppermute | solution.py:655
  33.9 0.0 copy-done.5
  34.0 0.0 copy-done.7
  34.0 0.0 copy-done.1
  34.0 0.0 copy-done.3
  34.0 5.8 %inner.1 = (f32[12,128,128]{2,1,0:T(8,128)}, f32[16,8,128]{2,1,0:T(8,128)S(1)}, f32[8,16,8,128]{3,2,1,0:T(8,128)S(1)}, f32[2,8,128]{2,1,0:T(8,128)S(1)}) custom-call(f32[8]{0:T(128)S(1)} %copy-done.9, f32[4]{0:T(128)S(1)} %copy-done.10, f32[3]{0:T(128)S(1)} %copy-done.11, f32[12,128,128]{2,1,0:T(8,128)S(1)} %bitcast.10, s32[4,128,128]{2,1,0:T(8,128)S(1)} %copy-done.3, ...), custom_call_target="tpu_custom_call" | custom-call | flops 134217728 | bytes 4194304 | tf_op jit(solution)/shard_map/inner/pallas_call | solution.py:607
  39.8 0.0 collective-permute-done.left
  39.8 0.0 collective-permute-done.1.right
  39.8 0.0 collective-permute-done.3.ends_other
  39.8 8.6 %edges.1 = (f32[12,128,128]{2,1,0:T(8,128)}, f32[16,2,8,128]{3,2,1,0:T(8,128)S(1)}, f32[4,8,128]{2,1,0:T(8,128)S(1)}, f32[6,8,128]{2,1,0:T(8,128)S(1)}, f32[8,6,8,128]{3,2,1,0:T(8,128)S(1)}) custom-call(f32[8]{0:T(128)S(1)} %copy-done.9, f32[4]{0:T(128)S(1)} %copy-done.10, f32[3]{0:T(128)S(1)} %copy-done.11, ...), custom_call_target="tpu_custom_call", output_to_operand_aliasing={{0}: (16, {})} | custom-call | bytes 4194304 | tf_op jit(solution)/shard_map/edges/pallas_call | solution.py:607
  48.4 17.8 %all_to_all.5.segments = f32[16,2,8,128]{3,2,1,0:T(8,128)S(1)} all-to-all(f32[16,2,8,128]{3,2,1,0:T(8,128)S(1)} %get-tuple-element.20), channel_id=1, replica_groups=mesh['corr'=16,'lc'=8] {'corr'}, dimensions={0} | all-to-all | bytes 262144 | tf_op jit(solution)/shard_map/all_to_all | solution.py:686
  66.2 0.8 %count.1 = f32[128,128]{1,0:T(8,128)} custom-call(f32[16,2,8,128]{3,2,1,0:T(8,128)S(1)} %all_to_all.5.segments, f32[4,8,128]{2,1,0:T(8,128)S(1)} %get-tuple-element.21.aux, f32[2,8,128]{2,1,0:T(8,128)S(1)} %get-tuple-element.17.inner, f32[16,8,128]{2,1,0:T(8,128)S(1)} %get-tuple-element.22.acc, f32[8,16,8,128]{3,2,1,0:T(8,128)S(1)} %get-tuple-element.23.low, ...), custom_call_target="tpu_custom_call" | custom-call | bytes 4194304 | tf_op jit(solution)/shard_map/count/pallas_call | solution.py:607
  (1 shorter events, 0.0 us)
Async XLA Ops:
  0.6 0.7 copy-start.12
  0.6 0.7 copy-start.13
  0.7 0.7 copy-start.14
  0.7 0.7 %copy-start.15 = (f32[128]{0:T(128)S(1)}, f32[128]{0:T(128)}, u32[]{:S(2)}) copy-start(f32[128]{0:T(128)} %param.20) | copy-start | bytes 1540
  0.7 0.7 %copy-start.9 = (f32[8]{0:T(128)S(1)}, f32[8]{0:T(128)}, u32[]{:S(2)}) copy-start(f32[8]{0:T(128)} %cap_table.5) | copy-start | bytes 100
  0.7 0.7 %copy-start.10 = (f32[4]{0:T(128)S(1)}, f32[4]{0:T(128)}, u32[]{:S(2)}) copy-start(f32[4]{0:T(128)} %jam_table.5) | copy-start | bytes 52
  0.7 0.7 %copy-start.11 = (f32[3]{0:T(128)S(1)}, f32[3]{0:T(128)}, u32[]{:S(2)}) copy-start(f32[3]{0:T(128)} %coef_ref.5) | copy-start | bytes 40
  1.4 1.1 %copy-start = (f32[4,3,128,128]{3,2,1,0:T(8,128)S(1)}, f32[4,3,128,128]{3,2,1,0:T(8,128)}, u32[]{:S(2)}) copy-start(f32[4,3,128,128]{3,2,1,0:T(8,128)} %param.12) | copy-start | bytes 2359300
  2.5 0.9 %copy-start.2 = (s32[4,128,128]{2,1,0:T(8,128)S(1)}, s32[4,128,128]{2,1,0:T(8,128)}, u32[]{:S(2)}) copy-start(s32[4,128,128]{2,1,0:T(8,128)} %c_hi.3) | copy-start | bytes 786436
  3.5 0.9 %copy-start.4 = (s32[4,128,128]{2,1,0:T(8,128)S(1)}, s32[4,128,128]{2,1,0:T(8,128)}, u32[]{:S(2)}) copy-start(s32[4,128,128]{2,1,0:T(8,128)} %j_hi.3) | copy-start | bytes 786436
  4.4 0.9 %copy-start.6 = (s32[3,128,128]{2,1,0:T(8,128)S(1)}, s32[3,128,128]{2,1,0:T(8,128)}, u32[]{:S(2)}) copy-start(s32[3,128,128]{2,1,0:T(8,128)} %a_hi.3) | copy-start | bytes 589828
  5.3 0.7 %copy-start.8 = (s32[8,4,128]{2,1,0:T(4,128)S(1)}, s32[8,4,128]{2,1,0:T(4,128)}, u32[]{:S(2)}) copy-start(s32[8,4,128]{2,1,0:T(4,128)} %param.16) | copy-start | bytes 49156
  6.1 27.9 %copy-start.5 = (s32[4,128,128]{2,1,0:T(8,128)S(1)}, s32[4,128,128]{2,1,0:T(8,128)}, u32[]{:S(2)}) copy-start(s32[4,128,128]{2,1,0:T(8,128)} %j_hi.3) | copy-start | bytes 786436
  6.1 27.9 %copy-start.7 = (s32[3,128,128]{2,1,0:T(8,128)S(1)}, s32[3,128,128]{2,1,0:T(8,128)}, u32[]{:S(2)}) copy-start(s32[3,128,128]{2,1,0:T(8,128)} %a_hi.3) | copy-start | bytes 589828
  7.0 27.0 %copy-start.1 = (f32[4,3,128,128]{3,2,1,0:T(8,128)S(1)}, f32[4,3,128,128]{3,2,1,0:T(8,128)}, u32[]{:S(2)}) copy-start(f32[4,3,128,128]{3,2,1,0:T(8,128)} %param.12) | copy-start | bytes 2359300
  7.0 9.7 %collective-permute-start.2 = (f32[152,128]{1,0:T(8,128)S(1)}, f32[152,128]{1,0:T(8,128)S(1)}, u32[]{:S(2)}, u32[]{:S(2)}) collective-permute-start(f32[152,128]{1,0:T(8,128)S(1)} %get-tuple-element.16), channel_id=1, source_target_pairs={{0,120},{120,0},{1,121},{121,1},{2,122},{122,2},{3,123},{123,3},{4... | collective-permute-start | bytes 233480 | tf_op jit(solution)/shard_map/ppermute | solution.py:653
  16.8 17.2 %copy-start.3 = (s32[4,128,128]{2,1,0:T(8,128)S(1)}, s32[4,128,128]{2,1,0:T(8,128)}, u32[]{:S(2)}) copy-start(s32[4,128,128]{2,1,0:T(8,128)} %c_hi.3) | copy-start | bytes 786436
  31.4 8.4 %collective-permute-start.3 = (f32[4,304,128]{2,1,0:T(8,128)S(1)}, f32[4,304,128]{2,1,0:T(8,128)S(1)}, u32[]{:S(2)}, u32[]{:S(2)}) collective-permute-start(f32[4,304,128]{2,1,0:T(8,128)S(1)} %bitcast.13), channel_id=1, source_target_pairs={{0,1},{1,0},{2,3},{3,2},{4,5},{5,4},{6,7},{7,6},{8,9},{9,8},{10,11... | collective-permute-start | bytes 1867784 | tf_op jit(solution)/shard_map/ppermute | solution.py:668
  31.4 8.4 %collective-permute-start = (f32[184,128]{1,0:T(8,128)S(1)}, f32[184,128]{1,0:T(8,128)S(1)}, u32[]{:S(2)}, u32[]{:S(2)}) collective-permute-start(f32[184,128]{1,0:T(8,128)S(1)} %get-tuple-element.14), channel_id=1, source_target_pairs={{0,8},{8,16},{16,24},{24,32},{32,40},{40,48},{48,56},{56,64},{64,7... | collective-permute-start | bytes 282632 | tf_op jit(solution)/shard_map/ppermute | solution.py:654
  32.6 7.1 %collective-permute-start.1 = (f32[184,128]{1,0:T(8,128)S(1)}, f32[184,128]{1,0:T(8,128)S(1)}, u32[]{:S(2)}, u32[]{:S(2)}) collective-permute-start(f32[184,128]{1,0:T(8,128)S(1)} %get-tuple-element.15), channel_id=1, source_target_pairs={{8,0},{16,8},{24,16},{32,24},{40,32},{48,40},{56,48},{64,56},{72,6... | collective-permute-start | bytes 282632 | tf_op jit(solution)/shard_map/ppermute | solution.py:655

commit v2 on v1

--- a/solution.py
+++ b/solution.py
@@ -15,7 +15,6 @@
 F32 = jnp.float32
 RAMP_UNIT = 0.01
 RAMP_FRACTION = (0.56, 0.16, 0.08)
-VMEM_BYTES = 40 * 1024 * 1024
 
 HEAD_DEPTH = 27
 TAIL_DEPTH = 35
@@ -154,7 +153,8 @@
     cap_table, jam_table, coef_ref, feed_a, feed_b, feed_a_row, feed_b_row, share_row, prio_row,
     ramp, d_lo, d_hi, c_lo, c_hi, j_lo, j_hi, a_lo, a_hi, fwd, bwd, zone,
 ):
-    tail = lax.axis_index("corr") == ROWS - 1
+    row_here = lax.axis_index("corr")
+    tail = row_here == ROWS - 1
     place = lax.axis_index("lc")
     for out, d, c, j, a in ((bwd, d_lo, c_lo, j_lo, a_lo), (fwd, d_hi, c_hi, j_hi, a_hi)):
         row = 0
@@ -234,6 +234,14 @@
     found = lax.fori_loop(0, WIDTH, note, jnp.zeros((8, WIDTH), jnp.int32), unroll=16)
     zone[pl.ds(INVERSE_ROW, 8), :] = found.astype(F32)
     zone[pl.ds(INVERSE_ROW + 8, 2), :] = jnp.zeros((2, WIDTH), F32)
+
+    @pl.when(tail)
+    def _():
+        fwd[pl.ds(0, RECORD), :] = zone[...]
+
+    @pl.when(row_here == 0)
+    def _():
+        bwd[pl.ds(0, RECORD), :] = zone[...]
 
 
 def inner_kernel(
@@ -420,7 +428,7 @@
 
 def edge_kernel(
     cap_table, jam_table, coef_ref, d_lo, d_hi, c_lo, c_hi, j_lo, j_hi, a_lo, a_hi, left, right,
-    ends_here, ends_other, inner, traffic_in, traffic, segment, aux, acc_out, low,
+    e0, e1, e2, e3, e4, e5, e6, e7, inner, traffic_in, traffic, segment, aux, acc_out, low,
     nat, zone, inj, spare_rows, st, tot, cap, jam, wave, adj, level, acc, out, sem,
 ):
     del traffic_in
@@ -432,16 +440,16 @@
 
     @pl.when(jnp.logical_or(first_row, last_row))
     def _():
-        for swap, ends in ((0, ends_here), (1, ends_other)):
-            core = jnp.where(swap == 0, place % 2, 1 - place % 2)
-            for z in range(4):
-                for m in range(2):
-                    side = jnp.where(first_row, m, 1 - m)
-                    base = side * (RECORD * 8) + 2 * z + core
-                    for r in range(RECORD // 8):
-                        zone[pl.ds(base + r * 64, 8, stride=8), :] = ends[
-                            z, pl.ds(m * RECORD + r * 8, 8), :
-                        ]
+        for n, ends in enumerate((e0, e1, e2, e3, e4, e5, e6, e7)):
+            chip = (place // 2 + (4 - n % 4)) % 4
+            core = place % 2 if n < 4 else 1 - place % 2
+            for m in range(2):
+                side = jnp.where(first_row, m, 1 - m)
+                base = side * (RECORD * 8) + 2 * chip + core
+                for r in range(RECORD // 8):
+                    zone[pl.ds(base + r * 64, 8, stride=8), :] = ends[
+                        pl.ds(m * RECORD + r * 8, 8), :
+                    ]
         junctions(place, zone, inj, spare_rows, cap_table, jam_table, coef)
 
     index = 0
@@ -603,7 +611,7 @@
 SCALARS = pl.BlockSpec(memory_space=pltpu.SMEM)
 
 
-def call(kernel, name, args, in_specs, outs, out_specs, scratch=(), aliases=None, flops=0):
+def call(kernel, name, args, in_specs, outs, out_specs, scratch=(), aliases=None, flops=0, vmem=32):
     return pl.pallas_call(
         kernel,
         grid=(1,),
@@ -612,7 +620,7 @@
         out_shape=outs,
         scratch_shapes=scratch,
         input_output_aliases=aliases or {},
-        compiler_params=pltpu.CompilerParams(vmem_limit_bytes=VMEM_BYTES),
+        compiler_params=pltpu.CompilerParams(vmem_limit_bytes=vmem << 20),
         cost_estimate=pl.CostEstimate(flops=flops, bytes_accessed=4 << 20, transcendentals=0),
         name=name,
     )(*args)
@@ -649,10 +657,17 @@
         [SCALARS] * 5 + [full(1, WIDTH)] * 4 + [full(32, WIDTH)] + specs,
         [shape(184, WIDTH), shape(184, WIDTH), shape(RECORD, WIDTH)],
         [full(184, WIDTH), full(184, WIDTH), full(RECORD, WIDTH)],
-    )
-    other_end = lax.ppermute(record, "corr", [(0, ROWS - 1), (ROWS - 1, 0)])
-    left = lax.ppermute(fwd, "corr", [(i, i + 1) for i in range(ROWS - 1)])
-    right = lax.ppermute(bwd, "corr", [(i + 1, i) for i in range(ROWS - 1)])
+        vmem=60,
+    )
+    left = lax.ppermute(fwd, "corr", [(i, (i + 1) % ROWS) for i in range(ROWS)])
+    right = lax.ppermute(bwd, "corr", [((i + 1) % ROWS, i) for i in range(ROWS)])
+    other_end = jnp.where(lax.axis_index("corr") == 0, left[:RECORD], right[:RECORD])
+    both = jnp.concatenate([record, other_end], 0)
+    both, left, right, density = lax.optimization_barrier((both, left, right, density))
+    grids[0] = density
+    pieces = [both] + [
+        lax.ppermute(both, "lc", [(i, (i + 2 * k) % 8) for i in range(8)]) for k in (1, 2, 3)
+    ]
     traffic, acc, low, inner = call(
         inner_kernel, "inner", tables + grids,
         [SCALARS] * 3 + [full(n, CELLS_HERE, WIDTH) for n in sizes],
@@ -661,17 +676,16 @@
         cells_scratch(16),
         flops=1 << 27,
     )
-    both = jnp.concatenate([record, other_end], 0)
-    ends_here = lax.all_gather(
-        both, "lc", axis_index_groups=[[0, 2, 4, 6], [1, 3, 5, 7]]
-    )
-    ends_other = lax.ppermute(ends_here, "lc", [(i, i ^ 1) for i in range(8)])
+    pieces = lax.optimization_barrier(tuple(pieces) + (inner,))
+    pieces, inner = list(pieces[:-1]), pieces[-1]
+    swap = [(i, i ^ 1) for i in range(8)]
+    pieces += [lax.ppermute(x, "lc", swap) for x in pieces]
     args, specs = ends(16)
     any_space = pl.BlockSpec(memory_space=pl.ANY)
     traffic, segment, aux, edge_acc, edge_low = call(
         edge_kernel, "edges",
-        tables + args + [left, right, ends_here, ends_other, inner, traffic],
-        [SCALARS] * 3 + specs + [full(184, WIDTH)] * 2 + [full(4, 2 * RECORD, WIDTH)] * 2
+        tables + args + [left, right] + pieces + [inner, traffic],
+        [SCALARS] * 3 + specs + [full(184, WIDTH)] * 2 + [full(2 * RECORD, WIDTH)] * 8
         + [full(2, 8, WIDTH), any_space],
         [shape(12, CELLS_HERE, WIDTH), shape(ROWS, 2, 8, WIDTH), shape(4, 8, WIDTH),
          shape(6, 8, WIDTH), shape(8, 6, 8, WIDTH)],
@@ -681,7 +695,7 @@
          pltpu.VMEM((STEPS * 12 * 8, WIDTH), F32), pltpu.VMEM((16, WIDTH), F32)]
         + cells_scratch(6)
         + [pltpu.VMEM((2, 12, 8, WIDTH), F32), pltpu.SemaphoreType.DMA((2,))],
-        aliases={16: 0},
+        aliases={22: 0},
     )
     segments = lax.all_to_all(segment, "corr", 0, 0)
     queue = call(

time: 67.4 us -> 51 us (0.76)
  blocking collectives: 32.4 us -> 14 us
  local copies, waits for them, and re-layouts: 5.39 us -> 0.03 us
  waiting for transfers between devices: 2.41 us -> 6.17 us
  starting transfers between devices: 9.91 us -> 11.8 us
  Pallas kernels: 16.1 us -> 17.2 us
  other arithmetic: 0.01 us -> 0.92 us
    all_gather x1 -> x0, blocking collectives: 14.6 us -> none  [on_device(): lax.all_gather(both, 'lc', axis_index_groups=[[0, 2, 4, 6], [1, 3, 5, 7]])]
    unnamed x32 -> x14, local copies, waits for them, and re-layouts: 5.39 us -> 0.03 us
    all_to_all x1, blocking collectives: 17.8 us -> 14 us  [on_device(): segments = lax.all_to_all(segment, 'corr', 0, 0)]
    ppermute x4 -> x9, waiting for transfers between devices: 2.41 us -> 6.17 us  [the longest x1 2.83 us: on_device(): left = lax.ppermute(fwd, 'corr', [(i, (i + 1) % ROWS) for i in range(ROWS)])]
    ppermute x4 -> x9, starting transfers between devices: 9.91 us -> 11.8 us  [the longest x3 5.37 us: on_device(): lax.ppermute(both, 'lc', [(i, (i + 2 * k) % 8) for i in range(8)])]
    pallas_call x4, Pallas kernels: 16.1 us -> 17.2 us  [call(): pl.pallas_call(kernel, grid=(1,), in_specs=in_specs, out_specs=out_specs,...]
    concatenate x1, other arithmetic: 0.01 us -> 0.91 us  [on_device(): both = jnp.concatenate([record, other_end], 0)]
  transfers between devices with their start and end apart: 4 -> 9, of which waited for: 1 -> 7; matrix products, arithmetic and copies ran while one was open for 0% -> 0% of each run, Pallas kernels for 9% -> 11%
where the time goes in v2:
time: 51 us; the launch traced here: 50.8 us
  Pallas kernels  17.2 us (34%)
  blocking collectives  14 us (27%)
  starting transfers between devices  11.8 us (23%)
  waiting for transfers between devices  6.17 us (12%)
  other arithmetic  0.92 us (2%)
  between operations  0.73 us (1%)
    pallas_call x4, Pallas kernels, call(): pl.pallas_call(kernel, grid=(1,), in_specs=in_specs, out_specs=out_specs,...  17.2 us
    all_to_all x1, blocking collectives, on_device(): segments = lax.all_to_all(segment, 'corr', 0, 0)  14 us
    ppermute x3, starting transfers between devices, on_device(): lax.ppermute(both, 'lc', [(i, (i + 2 * k) % 8) for i in range(8)])  5.37 us
    ppermute x1, starting transfers between devices, on_device(): lax.ppermute(bwd, 'corr', [((i + 1) % ROWS, i) for i in range(ROWS)])  3.8 us
    ppermute x1, waiting for transfers between devices, on_device(): left = lax.ppermute(fwd, 'corr', [(i, (i + 1) % ROWS) for i in range(ROWS)])  2.83 us
    ppermute x3, waiting for transfers between devices, on_device(): lax.ppermute(both, 'lc', [(i, (i + 2 * k) % 8) for i in range(8)])  2.23 us
    ppermute x1, starting transfers between devices, on_device(): left = lax.ppermute(fwd, 'corr', [(i, (i + 1) % ROWS) for i in range(ROWS)])  1.57 us
    ppermute x4, waiting for transfers between devices, on_device(): pieces += [lax.ppermute(x, 'lc', swap) for x in pieces]  1.09 us
  transfers between devices with their start and end apart: 9, of which 7 were waited for; matrix products, arithmetic and copies ran while one was open for 0% of the time, Pallas kernels for 11%

profile of v2, /device:TPU:0, one launch (start us, length us, event | category | flops | bytes accessed | tf_op | source)
XLA Modules:
  0.0 50.8 jit_solution(2864556383820307802)
XLA Ops:
  0.6 0.0 copy-start
  0.6 0.0 copy-start.3
  0.7 2.1 %pack.1 = (f32[184,128]{1,0:T(8,128)}, f32[184,128]{1,0:T(8,128)}, f32[152,128]{1,0:T(8,128)}) custom-call(f32[8]{0:T(128)} %cap_table.5, f32[4]{0:T(128)} %jam_table.5, f32[3]{0:T(128)} %coef_ref.5, s32[128]{0:T(128)} %feed_a.1, s32[128]{0:T(128)} %feed_b.1, s32[1,128]{1,0:T(1,128)} %bitcast.14, s32[1,128]{1,0:T(1,128)} %bitcast.15, f32[1,128]{1,0:T(1,128)} %bitcast.16, ...), custom_call_target="tpu_custom_call" | custom-call | bytes 4194304 | tf_op jit(solution)/shard_map/pack/pallas_call | solution.py:615
  2.7 1.6 %collective-permute-start = (f32[184,128]{1,0:T(8,128)}, f32[184,128]{1,0:T(8,128)S(1)}, u32[]{:S(2)}, u32[]{:S(2)}) collective-permute-start(f32[184,128]{1,0:T(8,128)} %get-tuple-element.24), channel_id=1, source_target_pairs={{0,8},{8,16},{16,24},{24,32},{32,40},{40,48},{48,56},{56,64},{64,7... | collective-permute-start | bytes 282632 | tf_op jit(solution)/shard_map/ppermute | solution.py:662
  4.3 3.8 %collective-permute-start.1 = (f32[184,128]{1,0:T(8,128)}, f32[184,128]{1,0:T(8,128)S(1)}, u32[]{:S(2)}, u32[]{:S(2)}) collective-permute-start(f32[184,128]{1,0:T(8,128)} %get-tuple-element.25), channel_id=1, source_target_pairs={{8,0},{16,8},{24,16},{32,24},{40,32},{48,40},{56,48},{64,56},{72,6... | collective-permute-start | bytes 282632 | tf_op jit(solution)/shard_map/ppermute | solution.py:663
  8.1 0.0 copy-start.1
  8.1 0.0 copy-start.2
  8.1 2.8 %collective-permute-done.left = f32[184,128]{1,0:T(8,128)S(1)} collective-permute-done((f32[184,128]{1,0:T(8,128)}, f32[184,128]{1,0:T(8,128)S(1)}, u32[]{:S(2)}, u32[]{:S(2)}) %collective-permute-start) | collective-permute-done | bytes 94240 | tf_op jit(solution)/shard_map/ppermute | solution.py:662
  10.9 0.0 collective-permute-done.1.right
  11.0 0.0 copy-start.4
  11.0 0.0 copy-start.5
  11.0 0.0 copy-start.6
  11.0 0.9 %pad_maximum_fusion.e0 = f32[304,128]{1,0:T(8,128)S(1)} fusion(f32[152,128]{1,0:T(8,128)S(1)} %slice_select_fusion, f32[152,128]{1,0:T(8,128)} %get-tuple-element.23), kind=kLoop, calls=%fused_computation | loop fusion | flops 38912 | bytes 311296 | tf_op jit(solution)/shard_map/concatenate | solution.py:665
  11.9 4.1 %collective-permute-start.4 = (f32[304,128]{1,0:T(8,128)S(1)}, f32[304,128]{1,0:T(8,128)S(1)}, u32[]{:S(2)}, u32[]{:S(2)}) collective-permute-start(f32[304,128]{1,0:T(8,128)S(1)} %pad_maximum_fusion.e0), channel_id=1, source_target_pairs={{0,6},{1,7},{2,0},{3,1},{4,2},{5,3},{6,4},{7,5},{8,14},{9,15},{10,... | collective-permute-start | bytes 466952 | tf_op jit(solution)/shard_map/ppermute | solution.py:669
  16.0 0.0 collective-permute-start.3
  16.0 1.3 %collective-permute-start.2 = (f32[304,128]{1,0:T(8,128)S(1)}, f32[304,128]{1,0:T(8,128)S(1)}, u32[]{:S(2)}, u32[]{:S(2)}) collective-permute-start(f32[304,128]{1,0:T(8,128)S(1)} %pad_maximum_fusion.e0), channel_id=1, source_target_pairs={{0,2},{1,3},{2,4},{3,5},{4,6},{5,7},{6,0},{7,1},{8,10},{9,11},{10,... | collective-permute-start | bytes 466952 | tf_op jit(solution)/shard_map/ppermute | solution.py:669
  17.3 0.0 copy-done
  17.3 0.0 copy-done.3
  17.3 0.0 copy-done.1
  17.3 0.0 copy-done.2
  17.3 0.0 copy-done.4
  17.3 0.0 copy-done.5
  17.3 0.0 copy-done.6
  17.3 5.8 %inner.1 = (f32[12,128,128]{2,1,0:T(8,128)}, f32[16,8,128]{2,1,0:T(8,128)S(1)}, f32[8,16,8,128]{3,2,1,0:T(8,128)S(1)}, f32[2,8,128]{2,1,0:T(8,128)S(1)}) custom-call(f32[8]{0:T(128)S(1)} %copy-done.4, f32[4]{0:T(128)S(1)} %copy-done.5, f32[3]{0:T(128)S(1)} %copy-done.6, f32[12,128,128]{2,1,0:T(8,128)S(1)} %bitcast.9, s32[4,128,128]{2,1,0:T(8,128)S(1)} %copy-done.1, ...), custom_call_target="tpu_custom_call" | custom-call | flops 134217728 | bytes 4194304 | tf_op jit(solution)/shard_map/inner/pallas_call | solution.py:615
  23.1 0.0 collective-permute-done.4.e3
  23.1 0.9 %collective-permute-done.3.e2 = f32[304,128]{1,0:T(8,128)S(1)} collective-permute-done((f32[304,128]{1,0:T(8,128)S(1)}, f32[304,128]{1,0:T(8,128)S(1)}, u32[]{:S(2)}, u32[]{:S(2)}) %collective-permute-start.3) | collective-permute-done | bytes 155680 | tf_op jit(solution)/shard_map/ppermute | solution.py:669
  24.1 1.3 %collective-permute-done.2.e1 = f32[304,128]{1,0:T(8,128)S(1)} collective-permute-done((f32[304,128]{1,0:T(8,128)S(1)}, f32[304,128]{1,0:T(8,128)S(1)}, u32[]{:S(2)}, u32[]{:S(2)}) %collective-permute-start.2) | collective-permute-done | bytes 155680 | tf_op jit(solution)/shard_map/ppermute | solution.py:669
  25.3 0.0 collective-permute-start.5
  25.3 0.5 collective-permute-start.6
  25.9 0.0 collective-permute-start.7
  25.9 0.5 collective-permute-start.8
  26.4 0.4 collective-permute-done.5.e4
  26.7 0.2 collective-permute-done.6.e5
  27.0 0.3 collective-permute-done.7.e6
  27.2 0.2 collective-permute-done.8.e7
  27.5 8.5 %edges.1 = (f32[12,128,128]{2,1,0:T(8,128)}, f32[16,2,8,128]{3,2,1,0:T(8,128)S(1)}, f32[4,8,128]{2,1,0:T(8,128)S(1)}, f32[6,8,128]{2,1,0:T(8,128)S(1)}, f32[8,6,8,128]{3,2,1,0:T(8,128)S(1)}) custom-call(f32[8]{0:T(128)S(1)} %copy-done.4, f32[4]{0:T(128)S(1)} %copy-done.5, f32[3]{0:T(128)S(1)} %copy-done.6, ...), custom_call_target="tpu_custom_call", output_to_operand_aliasing={{0}: (22, {})} | custom-call | bytes 4194304 | tf_op jit(solution)/shard_map/edges/pallas_call | solution.py:615
  36.0 14.0 %all_to_all.5.segments = f32[16,2,8,128]{3,2,1,0:T(8,128)S(1)} all-to-all(f32[16,2,8,128]{3,2,1,0:T(8,128)S(1)} %get-tuple-element.38), channel_id=1, replica_groups=mesh['corr'=16,'lc'=8] {'corr'}, dimensions={0} | all-to-all | bytes 262144 | tf_op jit(solution)/shard_map/all_to_all | solution.py:700
  50.0 0.8 %count.1 = f32[128,128]{1,0:T(8,128)} custom-call(f32[16,2,8,128]{3,2,1,0:T(8,128)S(1)} %all_to_all.5.segments, f32[4,8,128]{2,1,0:T(8,128)S(1)} %get-tuple-element.39.aux, f32[2,8,128]{2,1,0:T(8,128)S(1)} %get-tuple-element.35.inner, f32[16,8,128]{2,1,0:T(8,128)S(1)} %get-tuple-element.40.acc, f32[8,16,8,128]{3,2,1,0:T(8,128)S(1)} %get-tuple-element.41.low, ...), custom_call_target="tpu_custom_call" | custom-call | bytes 4194304 | tf_op jit(solution)/shard_map/count/pallas_call | solution.py:615
  (1 shorter events, 0.0 us)
Async XLA Ops:
  0.6 16.7 %copy-start = (f32[4,3,128,128]{3,2,1,0:T(8,128)S(1)}, f32[4,3,128,128]{3,2,1,0:T(8,128)}, u32[]{:S(2)}) copy-start(f32[4,3,128,128]{3,2,1,0:T(8,128)} %param.12) | copy-start | bytes 2359300
  0.6 16.6 %copy-start.3 = (s32[3,128,128]{2,1,0:T(8,128)S(1)}, s32[3,128,128]{2,1,0:T(8,128)}, u32[]{:S(2)}) copy-start(s32[3,128,128]{2,1,0:T(8,128)} %a_hi.3) | copy-start | bytes 589828
  2.7 8.2 %collective-permute-start = (f32[184,128]{1,0:T(8,128)}, f32[184,128]{1,0:T(8,128)S(1)}, u32[]{:S(2)}, u32[]{:S(2)}) collective-permute-start(f32[184,128]{1,0:T(8,128)} %get-tuple-element.24), channel_id=1, source_target_pairs={{0,8},{8,16},{16,24},{24,32},{32,40},{40,48},{48,56},{56,64},{64,7... | collective-permute-start | bytes 282632 | tf_op jit(solution)/shard_map/ppermute | solution.py:662
  4.3 6.6 %collective-permute-start.1 = (f32[184,128]{1,0:T(8,128)}, f32[184,128]{1,0:T(8,128)S(1)}, u32[]{:S(2)}, u32[]{:S(2)}) collective-permute-start(f32[184,128]{1,0:T(8,128)} %get-tuple-element.25), channel_id=1, source_target_pairs={{8,0},{16,8},{24,16},{32,24},{40,32},{48,40},{56,48},{64,56},{72,6... | collective-permute-start | bytes 282632 | tf_op jit(solution)/shard_map/ppermute | solution.py:663
  8.1 9.2 %copy-start.1 = (s32[4,128,128]{2,1,0:T(8,128)S(1)}, s32[4,128,128]{2,1,0:T(8,128)}, u32[]{:S(2)}) copy-start(s32[4,128,128]{2,1,0:T(8,128)} %c_hi.3) | copy-start | bytes 786436
  8.1 9.2 %copy-start.2 = (s32[4,128,128]{2,1,0:T(8,128)S(1)}, s32[4,128,128]{2,1,0:T(8,128)}, u32[]{:S(2)}) copy-start(s32[4,128,128]{2,1,0:T(8,128)} %j_hi.3) | copy-start | bytes 786436
  11.0 6.3 %copy-start.4 = (f32[8]{0:T(128)S(1)}, f32[8]{0:T(128)}, u32[]{:S(2)}) copy-start(f32[8]{0:T(128)} %cap_table.5) | copy-start | bytes 100
  11.0 6.3 %copy-start.5 = (f32[4]{0:T(128)S(1)}, f32[4]{0:T(128)}, u32[]{:S(2)}) copy-start(f32[4]{0:T(128)} %jam_table.5) | copy-start | bytes 52
  11.0 6.3 %copy-start.6 = (f32[3]{0:T(128)S(1)}, f32[3]{0:T(128)}, u32[]{:S(2)}) copy-start(f32[3]{0:T(128)} %coef_ref.5) | copy-start | bytes 40
  11.9 11.2 %collective-permute-start.4 = (f32[304,128]{1,0:T(8,128)S(1)}, f32[304,128]{1,0:T(8,128)S(1)}, u32[]{:S(2)}, u32[]{:S(2)}) collective-permute-start(f32[304,128]{1,0:T(8,128)S(1)} %pad_maximum_fusion.e0), channel_id=1, source_target_pairs={{0,6},{1,7},{2,0},{3,1},{4,2},{5,3},{6,4},{7,5},{8,14},{9,15},{10,... | collective-permute-start | bytes 466952 | tf_op jit(solution)/shard_map/ppermute | solution.py:669
  16.0 8.0 %collective-permute-start.3 = (f32[304,128]{1,0:T(8,128)S(1)}, f32[304,128]{1,0:T(8,128)S(1)}, u32[]{:S(2)}, u32[]{:S(2)}) collective-permute-start(f32[304,128]{1,0:T(8,128)S(1)} %pad_maximum_fusion.e0), channel_id=1, source_target_pairs={{0,4},{1,5},{2,6},{3,7},{4,0},{5,1},{6,2},{7,3},{8,12},{9,13},{10,... | collective-permute-start | bytes 466952 | tf_op jit(solution)/shard_map/ppermute | solution.py:669
  16.0 9.3 %collective-permute-start.2 = (f32[304,128]{1,0:T(8,128)S(1)}, f32[304,128]{1,0:T(8,128)S(1)}, u32[]{:S(2)}, u32[]{:S(2)}) collective-permute-start(f32[304,128]{1,0:T(8,128)S(1)} %pad_maximum_fusion.e0), channel_id=1, source_target_pairs={{0,2},{1,3},{2,4},{3,5},{4,6},{5,7},{6,0},{7,1},{8,10},{9,11},{10,... | collective-permute-start | bytes 466952 | tf_op jit(solution)/shard_map/ppermute | solution.py:669
  25.3 1.4 %collective-permute-start.5 = (f32[304,128]{1,0:T(8,128)S(1)}, f32[304,128]{1,0:T(8,128)S(1)}, u32[]{:S(2)}, u32[]{:S(2)}) collective-permute-start(f32[304,128]{1,0:T(8,128)S(1)} %pad_maximum_fusion.e0), channel_id=1, source_target_pairs={{0,1},{1,0},{2,3},{3,2},{4,5},{5,4},{6,7},{7,6},{8,9},{9,8},{10,11... | collective-permute-start | bytes 466952 | tf_op jit(solution)/shard_map/ppermute | solution.py:682
  25.3 1.6 %collective-permute-start.6 = (f32[304,128]{1,0:T(8,128)S(1)}, f32[304,128]{1,0:T(8,128)S(1)}, u32[]{:S(2)}, u32[]{:S(2)}) collective-permute-start(f32[304,128]{1,0:T(8,128)S(1)} %collective-permute-done.2.e1), channel_id=1, source_target_pairs={{0,1},{1,0},{2,3},{3,2},{4,5},{5,4},{6,7},{7,6},{8,9},{9,8},{10,11... | collective-permute-start | bytes 466952 | tf_op jit(solution)/shard_map/ppermute | solution.py:682
  25.9 1.4 %collective-permute-start.7 = (f32[304,128]{1,0:T(8,128)S(1)}, f32[304,128]{1,0:T(8,128)S(1)}, u32[]{:S(2)}, u32[]{:S(2)}) collective-permute-start(f32[304,128]{1,0:T(8,128)S(1)} %collective-permute-done.3.e2), channel_id=1, source_target_pairs={{0,1},{1,0},{2,3},{3,2},{4,5},{5,4},{6,7},{7,6},{8,9},{9,8},{10,11... | collective-permute-start | bytes 466952 | tf_op jit(solution)/shard_map/ppermute | solution.py:682
  25.9 1.6 %collective-permute-start.8 = (f32[304,128]{1,0:T(8,128)S(1)}, f32[304,128]{1,0:T(8,128)S(1)}, u32[]{:S(2)}, u32[]{:S(2)}) collective-permute-start(f32[304,128]{1,0:T(8,128)S(1)} %collective-permute-done.4.e3), channel_id=1, source_target_pairs={{0,1},{1,0},{2,3},{3,2},{4,5},{5,4},{6,7},{7,6},{8,9},{9,8},{10,11... | collective-permute-start | bytes 466952 | tf_op jit(solution)/shard_map/ppermute | solution.py:682

commit v3 on v2

--- a/solution.py
+++ b/solution.py
@@ -237,16 +237,16 @@
 
     @pl.when(tail)
     def _():
-        fwd[pl.ds(0, RECORD), :] = zone[...]
+        fwd[pl.ds(0, RECORD), :] = zone[pl.ds(0, RECORD), :]
 
     @pl.when(row_here == 0)
     def _():
-        bwd[pl.ds(0, RECORD), :] = zone[...]
+        bwd[pl.ds(0, RECORD), :] = zone[pl.ds(0, RECORD), :]
 
 
 def inner_kernel(
     cap_table, jam_table, coef_ref, density, cap_code, jam_code, adjacency,
-    traffic, acc_out, low, stats, st, tot, cap, jam, wave, adj, level, acc,
+    traffic, acc_out, low, stats, strip, st, tot, cap, jam, wave, adj, level, acc,
 ):
     coef = [coef_ref[k] for k in range(CLASSES)]
     fill(
@@ -257,6 +257,12 @@
         lambda i, rows: adjacency[i, rows, :].astype(F32),
         cap_table, jam_table,
     )
+    row = 0
+    for ref, n in ((density, 12), (cap_code, 4), (jam_code, 4), (adjacency, 3)):
+        for i in range(n):
+            strip[pl.ds(row * 32, 16), :] = ref[i, pl.ds(0, 16), :].astype(F32)
+            strip[pl.ds(row * 32 + 16, 16), :] = ref[i, pl.ds(CELLS_HERE - 16, 16), :].astype(F32)
+            row += 1
     sub = lax.broadcasted_iota(jnp.int32, (8, WIDTH), 0)
 
     def one(step, carry):
@@ -290,17 +296,99 @@
         acc_out[v] = acc[0, v]
 
 
-def junctions(near_here, zone, inj, spare_rows, cap_table, jam_table, coef):
-    head_row = lax.axis_index("corr") == 0
-
+def whole(x):
+    return x.astype(jnp.int32)
+
+
+def along(x, index, axis):
+    dims = lax.GatherDimensionNumbers(
+        offset_dims=(), collapsed_slice_dims=(axis,), start_index_map=(axis,),
+        operand_batching_dims=(1 - axis,), start_indices_batching_dims=(1 - axis,),
+    )
+    return lax.gather(
+        x, index[:, :, None], dims, (1, 1), mode=lax.GatherScatterMode.PROMISE_IN_BOUNDS
+    )
+
+
+def direct(index):
+    chunk = index >> 7
+    return index & (WIDTH - 1), [chunk == i for i in range(1, 8)]
+
+
+def permute_direct(x, how):
+    lane, masks = how
+    out = None
+    for i in range(8):
+        got = along(jnp.broadcast_to(x[i : i + 1, :], (8, WIDTH)), lane, 1)
+        out = got if out is None else jnp.where(masks[i - 1], got, out)
+    return out
+
+
+TURNS = 4
+FACTOR = (1, 1, 1, 3)
+RECIPROCAL = (1, 1, 1, 3)
+
+
+def offset(t, lane):
+    low, mid, high = lane & 7, (lane >> 3) & 7, lane >> 6
+    return (lane * 0, low, mid, 3 * low + 5 * mid + 4 * high)[t]
+
+
+def routed(indices, table):
+    n = len(indices)
+    for p, index in enumerate(indices):
+        table[pl.ds(8 * p, 8), :] = index
+    used = [jnp.zeros((n, WIDTH), jnp.int32) for _ in range(TURNS)]
+    fits = None
+    for i in range(8):
+        source = table[pl.ds(i, n, stride=8), :]
+        row, lane = source >> 7, source & (WIDTH - 1)
+        done = None
+        key = jnp.zeros((n, WIDTH), jnp.int32)
+        for t in range(TURNS):
+            slot = (FACTOR[t] * row + offset(t, lane)) & 7
+            bit = jnp.left_shift(jnp.ones((n, WIDTH), jnp.int32), slot)
+            free = (used[t] & bit) == 0
+            take = free if done is None else jnp.logical_and(free, jnp.logical_not(done))
+            used[t] = jnp.where(take, used[t] | bit, used[t])
+            key = jnp.where(take, 8 * t + slot, key)
+            done = take if done is None else jnp.logical_or(done, take)
+        fits = done if fits is None else jnp.logical_and(fits, done)
+        table[pl.ds(32 + i, n, stride=8), :] = key
+    sub = lax.broadcasted_iota(jnp.int32, (8, WIDTH), 0)
+    routes = []
+    for p, index in enumerate(indices):
+        key = table[pl.ds(32 + 8 * p, 8), :]
+        lane = index & (WIDTH - 1)
+        lanes = [jnp.zeros((8, WIDTH), jnp.int32) for _ in range(TURNS)]
+        for i in range(8):
+            where = jnp.broadcast_to(key[i : i + 1, :], (8, WIDTH)) - sub
+            what = jnp.broadcast_to(lane[i : i + 1, :], (8, WIDTH))
+            for t in range(TURNS):
+                lanes[t] = jnp.where(where == 8 * t, what, lanes[t])
+        turn = key >> 3
+        routes.append((lanes, key & 7, [turn == t for t in range(1, TURNS)]))
+    return routes, jnp.min(jnp.where(fits, 1.0, 0.0)) > 0.5
+
+
+def permute_routed(x, how):
+    lanes, slot, masks = how
+    sub = lax.broadcasted_iota(jnp.int32, (8, WIDTH), 0)
+    place = lax.broadcasted_iota(jnp.int32, (8, WIDTH), 1)
+    out = None
+    for t in range(TURNS):
+        y = x if t == 0 else along(x, (RECIPROCAL[t] * (sub - offset(t, place))) & 7, 0)
+        got = along(along(y, lanes[t], 1), slot, 0)
+        out = got if out is None else jnp.where(masks[t - 1], got, out)
+    return out
+
+
+def junctions(zone, inj, spare_rows, table, cap_table, jam_table, coef):
     def head(row):
         return zone[pl.ds(row * 8, 8), :]
 
     def tail(row):
         return zone[pl.ds((RECORD + row) * 8, 8), :]
-
-    def whole(x):
-        return x.astype(jnp.int32)
 
     feed_a = whole(head(FEED_ROW))
     feed_b = whole(tail(FEED_ROW))
@@ -314,23 +402,23 @@
     back_from_a = whole(spare_rows[pl.ds(0, 8), :])
     back_from_b = whole(spare_rows[pl.ds(8, 8), :])
 
-    def plan(index):
-        chunk = index // WIDTH
-        lane = index - chunk * WIDTH
-        return lane, [chunk == i for i in range(1, 8)]
-
-    plan_a, plan_b, plan_ra, plan_rb = (
-        plan(x) for x in (feed_a, feed_b, back_from_a, back_from_b)
-    )
-
-    def permute(x, how):
-        lane, masks = how
-        out = None
-        for i in range(8):
-            row = jnp.broadcast_to(x[i : i + 1, :], (8, WIDTH))
-            got = jnp.take_along_axis(row, lane, axis=1, mode="promise_in_bounds")
-            out = got if out is None else jnp.where(masks[i - 1], got, out)
-        return out
+    indices = (feed_a, feed_b, back_from_a, back_from_b)
+    routes, fits = routed(indices, table)
+    fixed = (head, tail, prio, share, inj, cap_table, jam_table, coef)
+
+    @pl.when(fits)
+    def _():
+        simulate(fixed, routes, permute_routed)
+
+    @pl.when(jnp.logical_not(fits))
+    def _():
+        simulate(fixed, [direct(x) for x in indices], permute_direct)
+
+
+def simulate(fixed, routes, permute):
+    head, tail, prio, share, inj, cap_table, jam_table, coef = fixed
+    head_row = lax.axis_index("corr") == 0
+    plan_a, plan_b, plan_ra, plan_rb = routes
 
     def statics(read, base):
         cap = [pick(whole(read(base + i)), cap_table, 8) for i in range(LANES)]
@@ -427,11 +515,10 @@
 
 
 def edge_kernel(
-    cap_table, jam_table, coef_ref, d_lo, d_hi, c_lo, c_hi, j_lo, j_hi, a_lo, a_hi, left, right,
-    e0, e1, e2, e3, e4, e5, e6, e7, inner, traffic_in, traffic, segment, aux, acc_out, low,
-    nat, zone, inj, spare_rows, st, tot, cap, jam, wave, adj, level, acc, out, sem,
+    cap_table, jam_table, coef_ref, strip, left, right,
+    e0, e1, e2, e3, e4, e5, e6, e7, inner, rim, segment, aux, acc_out, low,
+    nat, zone, inj, spare_rows, table, st, tot, cap, jam, wave, adj, level, acc,
 ):
-    del traffic_in
     row = lax.axis_index("corr")
     place = lax.axis_index("lc")
     coef = [coef_ref[k] for k in range(CLASSES)]
@@ -450,17 +537,12 @@
                     zone[pl.ds(base + r * 64, 8, stride=8), :] = ends[
                         pl.ds(m * RECORD + r * 8, 8), :
                     ]
-        junctions(place, zone, inj, spare_rows, cap_table, jam_table, coef)
-
-    index = 0
-    for n, lo, hi in ((12, d_lo, d_hi), (4, c_lo, c_hi), (4, j_lo, j_hi), (3, a_lo, a_hi)):
-        for i in range(n):
-            base = index * 48
-            nat[pl.ds(base, 8), :] = left[pl.ds(index * 8, 8), :]
-            nat[pl.ds(base + 8, 16), :] = lo[i].astype(F32)
-            nat[pl.ds(base + 24, 16), :] = hi[i].astype(F32)
-            nat[pl.ds(base + 40, 8), :] = right[pl.ds(index * 8, 8), :]
-            index += 1
+        junctions(zone, inj, spare_rows, table, cap_table, jam_table, coef)
+
+    for i in range(23):
+        nat[pl.ds(i * 48, 8), :] = left[pl.ds(i * 8, 8), :]
+        nat[pl.ds(i * 48 + 8, 32), :] = strip[pl.ds(i * 32, 32), :]
+        nat[pl.ds(i * 48 + 40, 8), :] = right[pl.ds(i * 8, 8), :]
 
     def rows_of(base):
         def read(i, rows):
@@ -531,14 +613,8 @@
             nat[pl.ds(i * 48 + v, 8, stride=6), :] = st[i, v]
         acc_out[v] = acc[0, v]
     for i in range(LANES * CLASSES):
-        out[0, i] = nat[pl.ds(i * 48 + 8, 8), :]
-        out[1, i] = nat[pl.ds(i * 48 + 32, 8), :]
-    copies = [
-        pltpu.make_async_copy(out.at[0], traffic.at[:, pl.ds(0, 8), :], sem.at[0]),
-        pltpu.make_async_copy(out.at[1], traffic.at[:, pl.ds(CELLS_HERE - 8, 8), :], sem.at[1]),
-    ]
-    for copy in copies:
-        copy.start()
+        rim[0, i] = nat[pl.ds(i * 48 + 8, 8), :]
+        rim[1, i] = nat[pl.ds(i * 48 + 32, 8), :]
     left_sum, left_low = aux[0], aux[1]
     most_sum = left_sum + inner[0]
     most_low = jnp.minimum(left_low, left_sum + inner[1])
@@ -547,13 +623,19 @@
     for i in range(ROWS):
         segment[i, 0] = all_sum
         segment[i, 1] = all_low
+
+
+def count_kernel(
+    segments, aux, inner, acc, low, edge_acc, edge_low, rim, traffic_in,
+    queue, traffic, sums, floors, nat, sem,
+):
+    del traffic_in
+    copies = [
+        pltpu.make_async_copy(rim.at[0], traffic.at[:, pl.ds(0, 8), :], sem.at[0]),
+        pltpu.make_async_copy(rim.at[1], traffic.at[:, pl.ds(CELLS_HERE - 8, 8), :], sem.at[1]),
+    ]
     for copy in copies:
-        copy.wait()
-
-
-def count_kernel(
-    segments, aux, inner, acc, low, edge_acc, edge_low, queue, sums, floors, nat
-):
+        copy.start()
     row = lax.axis_index("corr")
     total = jnp.zeros((8, WIDTH), F32)
     least = jnp.zeros((8, WIDTH), F32)
@@ -594,6 +676,8 @@
         nat[pl.ds(v, 8, stride=6), :] = value * scale
     queue[pl.ds(0, 8), :] = nat[pl.ds(8, 8), :]
     queue[pl.ds(CELLS_HERE - 8, 8), :] = nat[pl.ds(32, 8), :]
+    for copy in copies:
+        copy.wait()
 
 
 def shape(*dims):
@@ -609,12 +693,13 @@
 
 
 SCALARS = pl.BlockSpec(memory_space=pltpu.SMEM)
-
-
-def call(kernel, name, args, in_specs, outs, out_specs, scratch=(), aliases=None, flops=0, vmem=32):
+HERE = pl.BlockSpec(memory_space=pltpu.VMEM)
+
+
+def call(kernel, name, args, in_specs, outs, out_specs, scratch=(), aliases=None, flops=0, vmem=32, grid=(1,)):
     return pl.pallas_call(
         kernel,
-        grid=(1,),
+        grid=grid,
         in_specs=in_specs,
         out_specs=out_specs,
         out_shape=outs,
@@ -651,59 +736,62 @@
 
     args, specs = ends(8)
     line = [x.reshape(1, WIDTH) for x in (feed_a, feed_b, turn_share, priority)]
-    fwd, bwd, record = call(
+    fwd, bwd, both = call(
         pack_kernel, "pack",
         tables + [feed_a, feed_b] + line + [ramp_code.reshape(32, WIDTH)] + args,
         [SCALARS] * 5 + [full(1, WIDTH)] * 4 + [full(32, WIDTH)] + specs,
-        [shape(184, WIDTH), shape(184, WIDTH), shape(RECORD, WIDTH)],
-        [full(184, WIDTH), full(184, WIDTH), full(RECORD, WIDTH)],
+        [shape(184, WIDTH), shape(184, WIDTH), shape(2 * RECORD, WIDTH)],
+        [full(184, WIDTH), full(184, WIDTH), full(2 * RECORD, WIDTH)],
         vmem=60,
     )
     left = lax.ppermute(fwd, "corr", [(i, (i + 1) % ROWS) for i in range(ROWS)])
     right = lax.ppermute(bwd, "corr", [((i + 1) % ROWS, i) for i in range(ROWS)])
     other_end = jnp.where(lax.axis_index("corr") == 0, left[:RECORD], right[:RECORD])
-    both = jnp.concatenate([record, other_end], 0)
+    both = lax.dynamic_update_slice(both, other_end, (RECORD, 0))
     both, left, right, density = lax.optimization_barrier((both, left, right, density))
     grids[0] = density
     pieces = [both] + [
         lax.ppermute(both, "lc", [(i, (i + 2 * k) % 8) for i in range(8)]) for k in (1, 2, 3)
     ]
-    traffic, acc, low, inner = call(
+    traffic, acc, low, inner, strip = call(
         inner_kernel, "inner", tables + grids,
         [SCALARS] * 3 + [full(n, CELLS_HERE, WIDTH) for n in sizes],
-        [shape(12, CELLS_HERE, WIDTH), shape(16, 8, WIDTH), shape(8, 16, 8, WIDTH), shape(2, 8, WIDTH)],
-        [full(12, CELLS_HERE, WIDTH), full(16, 8, WIDTH), full(8, 16, 8, WIDTH), full(2, 8, WIDTH)],
+        [shape(12, CELLS_HERE, WIDTH), shape(16, 8, WIDTH), shape(8, 16, 8, WIDTH), shape(2, 8, WIDTH),
+         shape(23 * 32, WIDTH)],
+        [full(12, CELLS_HERE, WIDTH), full(16, 8, WIDTH), full(8, 16, 8, WIDTH), full(2, 8, WIDTH),
+         full(23 * 32, WIDTH)],
         cells_scratch(16),
         flops=1 << 27,
     )
-    pieces = lax.optimization_barrier(tuple(pieces) + (inner,))
-    pieces, inner = list(pieces[:-1]), pieces[-1]
     swap = [(i, i ^ 1) for i in range(8)]
-    pieces += [lax.ppermute(x, "lc", swap) for x in pieces]
-    args, specs = ends(16)
+    swapped = [lax.ppermute(both, "lc", swap)]
+    for n in (1, 2, 3):
+        pieces[n], inner = lax.optimization_barrier((pieces[n], inner))
+        swapped.append(lax.ppermute(pieces[n], "lc", swap))
+    pieces = pieces + swapped
     any_space = pl.BlockSpec(memory_space=pl.ANY)
-    traffic, segment, aux, edge_acc, edge_low = call(
+    rim, segment, aux, edge_acc, edge_low = call(
         edge_kernel, "edges",
-        tables + args + [left, right] + pieces + [inner, traffic],
-        [SCALARS] * 3 + specs + [full(184, WIDTH)] * 2 + [full(2 * RECORD, WIDTH)] * 8
-        + [full(2, 8, WIDTH), any_space],
-        [shape(12, CELLS_HERE, WIDTH), shape(ROWS, 2, 8, WIDTH), shape(4, 8, WIDTH),
+        tables + [strip, left, right] + pieces + [inner],
+        [SCALARS] * 3 + [HERE] * 12,
+        [shape(2, 12, 8, WIDTH), shape(ROWS, 2, 8, WIDTH), shape(4, 8, WIDTH),
          shape(6, 8, WIDTH), shape(8, 6, 8, WIDTH)],
-        [any_space, full(ROWS, 2, 8, WIDTH), full(4, 8, WIDTH), full(6, 8, WIDTH),
-         full(8, 6, 8, WIDTH)],
+        [HERE] * 5,
         [pltpu.VMEM((23 * 48, WIDTH), F32), pltpu.VMEM((2 * RECORD * 8, WIDTH), F32),
-         pltpu.VMEM((STEPS * 12 * 8, WIDTH), F32), pltpu.VMEM((16, WIDTH), F32)]
-        + cells_scratch(6)
-        + [pltpu.VMEM((2, 12, 8, WIDTH), F32), pltpu.SemaphoreType.DMA((2,))],
-        aliases={22: 0},
+         pltpu.VMEM((STEPS * 12 * 8, WIDTH), F32), pltpu.VMEM((16, WIDTH), F32),
+         pltpu.VMEM((64, WIDTH), jnp.int32)]
+        + cells_scratch(6),
+        grid=(),
     )
     segments = lax.all_to_all(segment, "corr", 0, 0)
-    queue = call(
-        count_kernel, "count", [segments, aux, inner, acc, low, edge_acc, edge_low],
-        [full(ROWS, 2, 8, WIDTH), full(4, 8, WIDTH), full(2, 8, WIDTH), full(16, 8, WIDTH),
-         full(8, 16, 8, WIDTH), full(6, 8, WIDTH), full(8, 6, 8, WIDTH)],
-        shape(CELLS_HERE, WIDTH), full(CELLS_HERE, WIDTH),
-        [pltpu.VMEM((3, 8, WIDTH), F32), pltpu.VMEM((3, 8, WIDTH), F32), pltpu.VMEM((48, WIDTH), F32)],
+    queue, traffic = call(
+        count_kernel, "count",
+        [segments, aux, inner, acc, low, edge_acc, edge_low, rim, traffic],
+        [HERE] * 8 + [any_space],
+        [shape(CELLS_HERE, WIDTH), shape(12, CELLS_HERE, WIDTH)], [HERE, any_space],
+        [pltpu.VMEM((3, 8, WIDTH), F32), pltpu.VMEM((3, 8, WIDTH), F32), pltpu.VMEM((48, WIDTH), F32),
+         pltpu.SemaphoreType.DMA((2,))],
+        aliases={8: 1}, grid=(),
     )
     return traffic.reshape(LANES, CLASSES, CELLS_HERE, WIDTH), queue
 

time: 51 us -> 49.7 us (0.975)
  waiting for transfers between devices: 6.17 us -> 3.94 us
  starting transfers between devices: 11.8 us -> 13 us
  Pallas kernels: 17.2 us -> 16.6 us
    ppermute x3, waiting for transfers between devices: 2.23 us -> 0.01 us  [on_device(): lax.ppermute(both, 'lc', [(i, (i + 2 * k) % 8) for i in range(8)])]
    ppermute x3, starting transfers between devices: 5.37 us -> 6.51 us  [on_device(): lax.ppermute(both, 'lc', [(i, (i + 2 * k) % 8) for i in range(8)])]
    concatenate x1 -> x0, other arithmetic: 0.91 us -> none  [on_device(): both = jnp.concatenate([record, other_end], 0)]
    dynamic_update_slice x0 -> x1, other arithmetic: none -> 0.63 us  [on_device(): both = lax.dynamic_update_slice(both, other_end, (RECORD, 0))]
    pallas_call x4, Pallas kernels: 17.2 us -> 16.6 us  [call(): pl.pallas_call(kernel, grid=grid, in_specs=in_specs, out_specs=out_specs,...]
  transfers between devices with their start and end apart: 9 -> 9, of which waited for: 7 -> 4; matrix products, arithmetic and copies ran while one was open for 0% -> 0% of each run, Pallas kernels for 11% -> 12%
where the time goes in v3:
time: 49.7 us; the launch traced here: 49.5 us
  Pallas kernels  16.6 us (33%)
  blocking collectives  14.5 us (29%)
  starting transfers between devices  13 us (26%)
  waiting for transfers between devices  3.94 us (8%)
  between operations  0.73 us (1%)
  other arithmetic  0.63 us (1%)
    pallas_call x4, Pallas kernels, call(): pl.pallas_call(kernel, grid=grid, in_specs=in_specs, out_specs=out_specs,...  16.6 us
    all_to_all x1, blocking collectives, on_device(): segments = lax.all_to_all(segment, 'corr', 0, 0)  14.5 us
    ppermute x3, starting transfers between devices, on_device(): lax.ppermute(both, 'lc', [(i, (i + 2 * k) % 8) for i in range(8)])  6.51 us
    ppermute x1, starting transfers between devices, on_device(): lax.ppermute(bwd, 'corr', [((i + 1) % ROWS, i) for i in range(ROWS)])  3.8 us
    ppermute x1, waiting for transfers between devices, on_device(): left = lax.ppermute(fwd, 'corr', [(i, (i + 1) % ROWS) for i in range(ROWS)])  2.83 us
    ppermute x1, starting transfers between devices, on_device(): left = lax.ppermute(fwd, 'corr', [(i, (i + 1) % ROWS) for i in range(ROWS)])  1.64 us
    ppermute x3, waiting for transfers between devices, on_device(): swapped.append(lax.ppermute(pieces[n], 'lc', swap))  1.09 us
    ppermute x3, starting transfers between devices, on_device(): swapped.append(lax.ppermute(pieces[n], 'lc', swap))  1.08 us
  transfers between devices with their start and end apart: 9, of which 4 were waited for; matrix products, arithmetic and copies ran while one was open for 0% of the time, Pallas kernels for 12%

profile of v3, /device:TPU:0, one launch (start us, length us, event | category | flops | bytes accessed | tf_op | source)
XLA Modules:
  0.0 49.5 jit_solution(16646120936031674033)
XLA Ops:
  0.6 0.0 copy-start
  0.6 0.0 copy-start.1
  0.7 0.0 copy-start.2
  0.7 2.1 %pack.1 = (f32[184,128]{1,0:T(8,128)}, f32[184,128]{1,0:T(8,128)}, f32[304,128]{1,0:T(8,128)}) custom-call(f32[8]{0:T(128)} %cap_table.5, f32[4]{0:T(128)} %jam_table.5, f32[3]{0:T(128)} %coef_ref.5, s32[128]{0:T(128)} %feed_a.1, s32[128]{0:T(128)} %feed_b.1, s32[1,128]{1,0:T(1,128)} %bitcast.12, s32[1,128]{1,0:T(1,128)} %bitcast.13, f32[1,128]{1,0:T(1,128)} %bitcast.14, ...), custom_call_target="tpu_custom_call" | custom-call | bytes 4194304 | tf_op jit(solution)/shard_map/pack/pallas_call | solution.py:700
  2.8 0.0 copy-start.3
  2.8 1.6 %collective-permute-start = (f32[184,128]{1,0:T(8,128)}, f32[184,128]{1,0:T(8,128)S(1)}, u32[]{:S(2)}, u32[]{:S(2)}) collective-permute-start(f32[184,128]{1,0:T(8,128)} %get-tuple-element.28), channel_id=1, source_target_pairs={{0,8},{8,16},{16,24},{24,32},{32,40},{40,48},{48,56},{56,64},{64,7... | collective-permute-start | bytes 282632 | tf_op jit(solution)/shard_map/ppermute | solution.py:747
  4.4 3.8 %collective-permute-start.1 = (f32[184,128]{1,0:T(8,128)}, f32[184,128]{1,0:T(8,128)S(1)}, u32[]{:S(2)}, u32[]{:S(2)}) collective-permute-start(f32[184,128]{1,0:T(8,128)} %get-tuple-element.29), channel_id=1, source_target_pairs={{8,0},{16,8},{24,16},{32,24},{40,32},{48,40},{56,48},{64,56},{72,6... | collective-permute-start | bytes 282632 | tf_op jit(solution)/shard_map/ppermute | solution.py:748
  8.2 2.8 %collective-permute-done.left = f32[184,128]{1,0:T(8,128)S(1)} collective-permute-done((f32[184,128]{1,0:T(8,128)}, f32[184,128]{1,0:T(8,128)S(1)}, u32[]{:S(2)}, u32[]{:S(2)}) %collective-permute-start) | collective-permute-done | bytes 94240 | tf_op jit(solution)/shard_map/ppermute | solution.py:747
  11.1 0.0 collective-permute-done.1.right
  11.1 0.0 copy-start.5
  11.1 0.0 copy-start.6
  11.1 0.0 copy-start.7
  11.1 0.6 %fusion.e0 = f32[304,128]{1,0:T(8,128)} fusion(f32[304,128]{1,0:T(8,128)} %get-tuple-element.27, f32[184,128]{1,0:T(8,128)S(1)} %collective-permute-done.1.right, f32[184,128]{1,0:T(8,128)S(1)} %collective-permute-done.left, pred[]{:T(512)S(6)} %eq.3), kind=kLoop, calls=%fused_computation.1 | loop fusion | flops 19456 | bytes 233473 | tf_op jit(solution)/shard_map/dynamic_update_slice | solution.py:750
  11.7 0.0 copy-start.4
  11.7 1.9 %collective-permute-start.2 = (f32[304,128]{1,0:T(8,128)}, f32[304,128]{1,0:T(8,128)S(1)}, u32[]{:S(2)}, u32[]{:S(2)}) collective-permute-start(f32[304,128]{1,0:T(8,128)} %fusion.e0), channel_id=1, source_target_pairs={{0,2},{1,3},{2,4},{3,5},{4,6},{5,7},{6,0},{7,1},{8,10},{9,11},{10,... | collective-permute-start | bytes 466952 | tf_op jit(solution)/shard_map/ppermute | solution.py:754
  13.6 3.6 %collective-permute-start.3 = (f32[304,128]{1,0:T(8,128)}, f32[304,128]{1,0:T(8,128)S(1)}, u32[]{:S(2)}, u32[]{:S(2)}) collective-permute-start(f32[304,128]{1,0:T(8,128)} %fusion.e0), channel_id=1, source_target_pairs={{0,4},{1,5},{2,6},{3,7},{4,0},{5,1},{6,2},{7,3},{8,12},{9,13},{10,... | collective-permute-start | bytes 466952 | tf_op jit(solution)/shard_map/ppermute | solution.py:754
  17.2 1.0 %collective-permute-start.4 = (f32[304,128]{1,0:T(8,128)}, f32[304,128]{1,0:T(8,128)S(1)}, u32[]{:S(2)}, u32[]{:S(2)}) collective-permute-start(f32[304,128]{1,0:T(8,128)} %fusion.e0), channel_id=1, source_target_pairs={{0,6},{1,7},{2,0},{3,1},{4,2},{5,3},{6,4},{7,5},{8,14},{9,15},{10,... | collective-permute-start | bytes 466952 | tf_op jit(solution)/shard_map/ppermute | solution.py:754
  18.2 0.0 collective-permute-start.5
  18.2 0.0 copy-done
  18.2 0.0 copy-done.1
  18.2 0.0 copy-done.2
  18.2 0.0 copy-done.3
  18.3 0.0 copy-done.5
  18.3 0.0 copy-done.6
  18.3 0.0 copy-done.7
  18.3 5.8 %inner.1 = (f32[12,128,128]{2,1,0:T(8,128)}, f32[16,8,128]{2,1,0:T(8,128)S(1)}, f32[8,16,8,128]{3,2,1,0:T(8,128)S(1)}, f32[2,8,128]{2,1,0:T(8,128)S(1)}, f32[736,128]{1,0:T(8,128)S(1)}) custom-call(f32[8]{0:T(128)S(1)} %copy-done.5, f32[4]{0:T(128)S(1)} %copy-done.6, f32[3]{0:T(128)S(1)} %copy-done.7, f32[12,128,128]{2,1,0:T(8,128)S(1)} %bitcast.9, ...), custom_call_target="tpu_custom_call" | custom-call | flops 134217728 | bytes 4194304 | tf_op jit(solution)/shard_map/inner/pallas_call | solution.py:700
  24.1 0.0 collective-permute-done.2.e1
  24.1 0.0 collective-permute-done.3.e2
  24.1 0.0 collective-permute-done.4.e3
  24.1 0.6 %collective-permute-start.8 = (f32[304,128]{1,0:T(8,128)S(1)}, f32[304,128]{1,0:T(8,128)S(1)}, u32[]{:S(2)}, u32[]{:S(2)}) collective-permute-start(f32[304,128]{1,0:T(8,128)S(1)} %collective-permute-done.4.e3), channel_id=1, source_target_pairs={{0,1},{1,0},{2,3},{3,2},{4,5},{5,4},{6,7},{7,6},{8,9},{9,8},{10,11... | collective-permute-start | bytes 466952 | tf_op jit(solution)/shard_map/ppermute | solution.py:770
  24.7 0.1 collective-permute-start.7
  24.8 0.4 collective-permute-start.6
  25.2 0.0 collective-permute-done.5.e4
  25.2 0.5 %collective-permute-done.8.e7 = f32[304,128]{1,0:T(8,128)S(1)} collective-permute-done((f32[304,128]{1,0:T(8,128)S(1)}, f32[304,128]{1,0:T(8,128)S(1)}, u32[]{:S(2)}, u32[]{:S(2)}) %collective-permute-start.8) | collective-permute-done | bytes 155680 | tf_op jit(solution)/shard_map/ppermute | solution.py:770
  25.7 0.4 collective-permute-done.7.e6
  26.1 0.2 collective-permute-done.6.e5
  26.3 0.0 copy-done.4
  26.3 7.4 %edges.1 = (f32[2,12,8,128]{3,2,1,0:T(8,128)S(1)}, f32[16,2,8,128]{3,2,1,0:T(8,128)S(1)}, f32[4,8,128]{2,1,0:T(8,128)S(1)}, f32[6,8,128]{2,1,0:T(8,128)S(1)}, f32[8,6,8,128]{3,2,1,0:T(8,128)S(1)}) custom-call(f32[8]{0:T(128)S(1)} %copy-done.5, f32[4]{0:T(128)S(1)} %copy-done.6, f32[3]{0:T(128)S(1)} %copy-done.7, f32[736,128]{1,0:T(8,128)S(1)} %get-tuple-element.31.strip, ...), custom_call_target="tpu_custom_call" | custom-call | bytes 4194304 | tf_op jit(solution)/shard_map/edges/pallas_call | solution.py:700
  33.7 14.5 %all_to_all.5.segments = f32[16,2,8,128]{3,2,1,0:T(8,128)S(1)} all-to-all(f32[16,2,8,128]{3,2,1,0:T(8,128)S(1)} %get-tuple-element.42), channel_id=1, replica_groups=mesh['corr'=16,'lc'=8] {'corr'}, dimensions={0} | all-to-all | bytes 262144 | tf_op jit(solution)/shard_map/all_to_all | solution.py:786
  48.2 1.3 %count.1 = (f32[128,128]{1,0:T(8,128)}, f32[12,128,128]{2,1,0:T(8,128)}) custom-call(f32[16,2,8,128]{3,2,1,0:T(8,128)S(1)} %all_to_all.5.segments, f32[4,8,128]{2,1,0:T(8,128)S(1)} %get-tuple-element.43.aux, f32[2,8,128]{2,1,0:T(8,128)S(1)} %get-tuple-element.41.inner, f32[16,8,128]{2,1,0:T(8,128)S(1)} %get-tuple-element.44.acc, ...), custom_call_target="tpu_custom_call", output_to_operand_aliasing={{1}: (8, {})} | custom-call | bytes 4194304 | tf_op jit(solution)/shard_map/count/pallas_call | solution.py:700
Async XLA Ops:
  0.6 17.6 %copy-start = (f32[4,3,128,128]{3,2,1,0:T(8,128)S(1)}, f32[4,3,128,128]{3,2,1,0:T(8,128)}, u32[]{:S(2)}) copy-start(f32[4,3,128,128]{3,2,1,0:T(8,128)} %param.12) | copy-start | bytes 2359300
  0.6 17.6 %copy-start.1 = (s32[4,128,128]{2,1,0:T(8,128)S(1)}, s32[4,128,128]{2,1,0:T(8,128)}, u32[]{:S(2)}) copy-start(s32[4,128,128]{2,1,0:T(8,128)} %cap_code.1) | copy-start | bytes 786436
  0.7 17.6 %copy-start.2 = (s32[4,128,128]{2,1,0:T(8,128)S(1)}, s32[4,128,128]{2,1,0:T(8,128)}, u32[]{:S(2)}) copy-start(s32[4,128,128]{2,1,0:T(8,128)} %jam_code.1) | copy-start | bytes 786436
  2.8 15.5 %copy-start.3 = (s32[3,128,128]{2,1,0:T(8,128)S(1)}, s32[3,128,128]{2,1,0:T(8,128)}, u32[]{:S(2)}) copy-start(s32[3,128,128]{2,1,0:T(8,128)} %adjacency.1) | copy-start | bytes 589828
  2.8 8.3 %collective-permute-start = (f32[184,128]{1,0:T(8,128)}, f32[184,128]{1,0:T(8,128)S(1)}, u32[]{:S(2)}, u32[]{:S(2)}) collective-permute-start(f32[184,128]{1,0:T(8,128)} %get-tuple-element.28), channel_id=1, source_target_pairs={{0,8},{8,16},{16,24},{24,32},{32,40},{40,48},{48,56},{56,64},{64,7... | collective-permute-start | bytes 282632 | tf_op jit(solution)/shard_map/ppermute | solution.py:747
  4.4 6.6 %collective-permute-start.1 = (f32[184,128]{1,0:T(8,128)}, f32[184,128]{1,0:T(8,128)S(1)}, u32[]{:S(2)}, u32[]{:S(2)}) collective-permute-start(f32[184,128]{1,0:T(8,128)} %get-tuple-element.29), channel_id=1, source_target_pairs={{8,0},{16,8},{24,16},{32,24},{40,32},{48,40},{56,48},{64,56},{72,6... | collective-permute-start | bytes 282632 | tf_op jit(solution)/shard_map/ppermute | solution.py:748
  11.1 7.2 %copy-start.5 = (f32[8]{0:T(128)S(1)}, f32[8]{0:T(128)}, u32[]{:S(2)}) copy-start(f32[8]{0:T(128)} %cap_table.5) | copy-start | bytes 100
  11.1 7.2 %copy-start.6 = (f32[4]{0:T(128)S(1)}, f32[4]{0:T(128)}, u32[]{:S(2)}) copy-start(f32[4]{0:T(128)} %jam_table.5) | copy-start | bytes 52
  11.1 7.2 %copy-start.7 = (f32[3]{0:T(128)S(1)}, f32[3]{0:T(128)}, u32[]{:S(2)}) copy-start(f32[3]{0:T(128)} %coef_ref.5) | copy-start | bytes 40
  11.7 14.6 %copy-start.4 = (f32[304,128]{1,0:T(8,128)S(1)}, f32[304,128]{1,0:T(8,128)}, u32[]{:S(2)}) copy-start(f32[304,128]{1,0:T(8,128)} %fusion.e0) | copy-start | bytes 466948
  11.7 12.4 %collective-permute-start.2 = (f32[304,128]{1,0:T(8,128)}, f32[304,128]{1,0:T(8,128)S(1)}, u32[]{:S(2)}, u32[]{:S(2)}) collective-permute-start(f32[304,128]{1,0:T(8,128)} %fusion.e0), channel_id=1, source_target_pairs={{0,2},{1,3},{2,4},{3,5},{4,6},{5,7},{6,0},{7,1},{8,10},{9,11},{10,... | collective-permute-start | bytes 466952 | tf_op jit(solution)/shard_map/ppermute | solution.py:754
  13.6 10.5 %collective-permute-start.3 = (f32[304,128]{1,0:T(8,128)}, f32[304,128]{1,0:T(8,128)S(1)}, u32[]{:S(2)}, u32[]{:S(2)}) collective-permute-start(f32[304,128]{1,0:T(8,128)} %fusion.e0), channel_id=1, source_target_pairs={{0,4},{1,5},{2,6},{3,7},{4,0},{5,1},{6,2},{7,3},{8,12},{9,13},{10,... | collective-permute-start | bytes 466952 | tf_op jit(solution)/shard_map/ppermute | solution.py:754
  17.2 6.9 %collective-permute-start.4 = (f32[304,128]{1,0:T(8,128)}, f32[304,128]{1,0:T(8,128)S(1)}, u32[]{:S(2)}, u32[]{:S(2)}) collective-permute-start(f32[304,128]{1,0:T(8,128)} %fusion.e0), channel_id=1, source_target_pairs={{0,6},{1,7},{2,0},{3,1},{4,2},{5,3},{6,4},{7,5},{8,14},{9,15},{10,... | collective-permute-start | bytes 466952 | tf_op jit(solution)/shard_map/ppermute | solution.py:754
  18.2 7.0 %collective-permute-start.5 = (f32[304,128]{1,0:T(8,128)}, f32[304,128]{1,0:T(8,128)S(1)}, u32[]{:S(2)}, u32[]{:S(2)}) collective-permute-start(f32[304,128]{1,0:T(8,128)} %fusion.e0), channel_id=1, source_target_pairs={{0,1},{1,0},{2,3},{3,2},{4,5},{5,4},{6,7},{7,6},{8,9},{9,8},{10,11... | collective-permute-start | bytes 466952 | tf_op jit(solution)/shard_map/ppermute | solution.py:767
  24.1 1.6 %collective-permute-start.8 = (f32[304,128]{1,0:T(8,128)S(1)}, f32[304,128]{1,0:T(8,128)S(1)}, u32[]{:S(2)}, u32[]{:S(2)}) collective-permute-start(f32[304,128]{1,0:T(8,128)S(1)} %collective-permute-done.4.e3), channel_id=1, source_target_pairs={{0,1},{1,0},{2,3},{3,2},{4,5},{5,4},{6,7},{7,6},{8,9},{9,8},{10,11... | collective-permute-start | bytes 466952 | tf_op jit(solution)/shard_map/ppermute | solution.py:770
  24.7 1.4 %collective-permute-start.7 = (f32[304,128]{1,0:T(8,128)S(1)}, f32[304,128]{1,0:T(8,128)S(1)}, u32[]{:S(2)}, u32[]{:S(2)}) collective-permute-start(f32[304,128]{1,0:T(8,128)S(1)} %collective-permute-done.3.e2), channel_id=1, source_target_pairs={{0,1},{1,0},{2,3},{3,2},{4,5},{5,4},{6,7},{7,6},{8,9},{9,8},{10,11... | collective-permute-start | bytes 466952 | tf_op jit(solution)/shard_map/ppermute | solution.py:770
  24.8 1.5 %collective-permute-start.6 = (f32[304,128]{1,0:T(8,128)S(1)}, f32[304,128]{1,0:T(8,128)S(1)}, u32[]{:S(2)}, u32[]{:S(2)}) collective-permute-start(f32[304,128]{1,0:T(8,128)S(1)} %collective-permute-done.2.e1), channel_id=1, source_target_pairs={{0,1},{1,0},{2,3},{3,2},{4,5},{5,4},{6,7},{7,6},{8,9},{9,8},{10,11... | collective-permute-start | bytes 466952 | tf_op jit(solution)/shard_map/ppermute | solution.py:770

commit v4 on v3

--- a/solution.py
+++ b/solution.py
@@ -6,6 +6,7 @@
 from jax.sharding import PartitionSpec as P
 
 STEPS = 8
+HALF = 4
 LANES = 4
 CLASSES = 3
 ROWS = 16
@@ -129,7 +130,7 @@
 
 def fill(count, stride, refs, density, cap_code, jam_code, adjacency, cap_table, jam_table):
     st, tot, cap, jam, wave, adj, level, acc = refs
-    for v in range(count):
+    def one(v, carry):
         rows = pl.ds(v, 8, stride=stride)
         around = None
         for lane in range(LANES):
@@ -147,6 +148,9 @@
             adj[p, v] = adjacency(p, rows)
         level[v] = 0.5 * around
         acc[0, v] = jnp.zeros((8, WIDTH), F32)
+        return carry
+
+    lax.fori_loop(0, count, one, 0)
 
 
 def pack_kernel(
@@ -244,25 +248,7 @@
         bwd[pl.ds(0, RECORD), :] = zone[pl.ds(0, RECORD), :]
 
 
-def inner_kernel(
-    cap_table, jam_table, coef_ref, density, cap_code, jam_code, adjacency,
-    traffic, acc_out, low, stats, strip, st, tot, cap, jam, wave, adj, level, acc,
-):
-    coef = [coef_ref[k] for k in range(CLASSES)]
-    fill(
-        16, 16, (st, tot, cap, jam, wave, adj, level, acc),
-        lambda i, rows: density[i, rows, :],
-        lambda i, rows: cap_code[i, rows, :],
-        lambda i, rows: jam_code[i, rows, :],
-        lambda i, rows: adjacency[i, rows, :].astype(F32),
-        cap_table, jam_table,
-    )
-    row = 0
-    for ref, n in ((density, 12), (cap_code, 4), (jam_code, 4), (adjacency, 3)):
-        for i in range(n):
-            strip[pl.ds(row * 32, 16), :] = ref[i, pl.ds(0, 16), :].astype(F32)
-            strip[pl.ds(row * 32 + 16, 16), :] = ref[i, pl.ds(CELLS_HERE - 16, 16), :].astype(F32)
-            row += 1
+def inner_steps(begin, end, coef, refs, stats):
     sub = lax.broadcasted_iota(jnp.int32, (8, WIDTH), 0)
 
     def one(step, carry):
@@ -282,14 +268,55 @@
             )
 
         window(
-            16, (st, tot, cap, jam, wave, adj, level, acc, low), step, coef,
+            16, refs, step, coef,
             lambda v, before, leaving: (before, leaving),
             lambda v: (sub != 0) if v < 8 else (sub != 7),
             scan,
         )
         return carry
 
-    lax.fori_loop(0, STEPS, one, 0)
+    lax.fori_loop(begin, end, one, 0)
+
+
+def early_kernel(
+    cap_table, jam_table, coef_ref, density, cap_code, jam_code, adjacency,
+    low, stats, strip, st, tot, cap, jam, wave, adj, level, acc,
+):
+    coef = [coef_ref[k] for k in range(CLASSES)]
+    fill(
+        16, 16, (st, tot, cap, jam, wave, adj, level, acc),
+        lambda i, rows: density[i, rows, :],
+        lambda i, rows: cap_code[i, rows, :],
+        lambda i, rows: jam_code[i, rows, :],
+        lambda i, rows: adjacency[i, rows, :].astype(F32),
+        cap_table, jam_table,
+    )
+    row = 0
+    for ref, n in ((density, 12), (cap_code, 4), (jam_code, 4), (adjacency, 3)):
+        for i in range(n):
+            strip[pl.ds(row * 32, 16), :] = ref[i, pl.ds(0, 16), :].astype(F32)
+            strip[pl.ds(row * 32 + 16, 16), :] = ref[i, pl.ds(CELLS_HERE - 16, 16), :].astype(F32)
+            row += 1
+    inner_steps(
+        0, HALF, coef, (st, tot, cap, jam, wave, adj, level, acc, low), stats
+    )
+
+
+def late_kernel(
+    coef_ref, early_stats, st_in, tot_in, cap, jam, wave, adj, level, acc_in,
+    traffic, acc_out, low, stats, st, tot, acc,
+):
+    coef = [coef_ref[k] for k in range(CLASSES)]
+    stats[...] = early_stats[...]
+    for v in range(16):
+        for i in range(LANES * CLASSES):
+            st[i, v] = st_in[i, v]
+        for i in range(LANES):
+            tot[i, v] = tot_in[i, v]
+        acc[0, v] = acc_in[0, v]
+    inner_steps(
+        HALF, STEPS, coef, (st, tot, cap, jam, wave, adj, level, acc, low), stats
+    )
     for v in range(16):
         for i in range(LANES * CLASSES):
             traffic[i, pl.ds(v, 8, stride=16), :] = st[i, v]
@@ -626,7 +653,7 @@
 
 
 def count_kernel(
-    segments, aux, inner, acc, low, edge_acc, edge_low, rim, traffic_in,
+    segments, aux, inner, acc, early_low, late_low, edge_acc, edge_low, rim, traffic_in,
     queue, traffic, sums, floors, nat, sem,
 ):
     del traffic_in
@@ -660,7 +687,7 @@
     for v in range(16):
         value = acc[v]
         for s in range(STEPS):
-            value = value + (inside[s][0] - jnp.minimum(inside[s][1], inside[s][0] + low[s, v]))
+            value = value + (inside[s][0] - jnp.minimum(inside[s][1], inside[s][0] + (early_low if s < HALF else late_low)[s, v]))
         queue[pl.ds(v, 8, stride=16), :] = value * scale
     edges = [
         (
@@ -746,22 +773,33 @@
     )
     left = lax.ppermute(fwd, "corr", [(i, (i + 1) % ROWS) for i in range(ROWS)])
     right = lax.ppermute(bwd, "corr", [((i + 1) % ROWS, i) for i in range(ROWS)])
+    def cells(n):
+        return (n, 16, 8, WIDTH)
+
+    held = [cells(12), cells(4), cells(4), cells(4), cells(4), cells(3), (16, 8, WIDTH), cells(2)]
+    early_low, inner, strip, *state = call(
+        early_kernel, "early", tables + grids,
+        [SCALARS] * 3 + [full(n, CELLS_HERE, WIDTH) for n in sizes],
+        [shape(8, 16, 8, WIDTH), shape(2, 8, WIDTH), shape(23 * 32, WIDTH)]
+        + [shape(*x) for x in held],
+        [full(8, 16, 8, WIDTH), full(2, 8, WIDTH), full(23 * 32, WIDTH)]
+        + [full(*x) for x in held],
+        flops=1 << 26,
+    )
+    left, right, inner = lax.optimization_barrier((left, right, inner))
     other_end = jnp.where(lax.axis_index("corr") == 0, left[:RECORD], right[:RECORD])
     both = lax.dynamic_update_slice(both, other_end, (RECORD, 0))
-    both, left, right, density = lax.optimization_barrier((both, left, right, density))
-    grids[0] = density
+    both, state = lax.optimization_barrier((both, tuple(state)))
     pieces = [both] + [
         lax.ppermute(both, "lc", [(i, (i + 2 * k) % 8) for i in range(8)]) for k in (1, 2, 3)
     ]
-    traffic, acc, low, inner, strip = call(
-        inner_kernel, "inner", tables + grids,
-        [SCALARS] * 3 + [full(n, CELLS_HERE, WIDTH) for n in sizes],
-        [shape(12, CELLS_HERE, WIDTH), shape(16, 8, WIDTH), shape(8, 16, 8, WIDTH), shape(2, 8, WIDTH),
-         shape(23 * 32, WIDTH)],
-        [full(12, CELLS_HERE, WIDTH), full(16, 8, WIDTH), full(8, 16, 8, WIDTH), full(2, 8, WIDTH),
-         full(23 * 32, WIDTH)],
-        cells_scratch(16),
-        flops=1 << 27,
+    traffic, acc, late_low, inner = call(
+        late_kernel, "late", [change_coef, inner] + list(state),
+        [SCALARS, full(2, 8, WIDTH)] + [full(*x) for x in held],
+        [shape(12, CELLS_HERE, WIDTH), shape(16, 8, WIDTH), shape(8, 16, 8, WIDTH), shape(2, 8, WIDTH)],
+        [full(12, CELLS_HERE, WIDTH), full(16, 8, WIDTH), full(8, 16, 8, WIDTH), full(2, 8, WIDTH)],
+        [pltpu.VMEM(cells(12), F32), pltpu.VMEM(cells(4), F32), pltpu.VMEM(cells(2), F32)],
+        flops=1 << 26,
     )
     swap = [(i, i ^ 1) for i in range(8)]
     swapped = [lax.ppermute(both, "lc", swap)]
@@ -786,12 +824,12 @@
     segments = lax.all_to_all(segment, "corr", 0, 0)
     queue, traffic = call(
         count_kernel, "count",
-        [segments, aux, inner, acc, low, edge_acc, edge_low, rim, traffic],
-        [HERE] * 8 + [any_space],
+        [segments, aux, inner, acc, early_low, late_low, edge_acc, edge_low, rim, traffic],
+        [HERE] * 9 + [any_space],
         [shape(CELLS_HERE, WIDTH), shape(12, CELLS_HERE, WIDTH)], [HERE, any_space],
         [pltpu.VMEM((3, 8, WIDTH), F32), pltpu.VMEM((3, 8, WIDTH), F32), pltpu.VMEM((48, WIDTH), F32),
          pltpu.SemaphoreType.DMA((2,))],
-        aliases={8: 1}, grid=(),
+        aliases={9: 1}, grid=(),
     )
     return traffic.reshape(LANES, CLASSES, CELLS_HERE, WIDTH), queue
 

time: 49.7 us -> 47.8 us (0.962)
  blocking collectives: 14.5 us -> 12.5 us
  Pallas kernels: 16.6 us -> 17.6 us
  local copies, waits for them, and re-layouts: 0.03 us -> 0.67 us
  other arithmetic: 0.63 us -> 0.02 us
  starting transfers between devices: 13 us -> 12.5 us
    ppermute x1, waiting for transfers between devices: 2.83 us -> 0.01 us  [on_device(): left = lax.ppermute(fwd, 'corr', [(i, (i + 1) % ROWS) for i in range(ROWS)])]
    ppermute x3, waiting for transfers between devices: 0.01 us -> 2.17 us  [on_device(): lax.ppermute(both, 'lc', [(i, (i + 2 * k) % 8) for i in range(8)])]
    all_to_all x1, blocking collectives: 14.5 us -> 12.5 us  [on_device(): segments = lax.all_to_all(segment, 'corr', 0, 0)]
    pallas_call x4 -> x5, Pallas kernels: 16.6 us -> 17.6 us  [call(): pl.pallas_call(kernel, grid=grid, in_specs=in_specs, out_specs=out_specs,...]
    unnamed x16, local copies, waits for them, and re-layouts: 0.03 us -> 0.67 us
    dynamic_update_slice x1, other arithmetic: 0.63 us -> 0.02 us  [on_device(): both = lax.dynamic_update_slice(both, other_end, (RECORD, 0))]
    ppermute x3, starting transfers between devices: 1.08 us -> 0.51 us  [on_device(): swapped.append(lax.ppermute(pieces[n], 'lc', swap))]
  transfers between devices with their start and end apart: 9 -> 9, of which waited for: 4 -> 4; matrix products, arithmetic and copies ran while one was open for 0% -> 0% of each run, Pallas kernels for 12% -> 14%
where the time goes in v4:
time: 47.8 us; the launch traced here: 47.6 us
  Pallas kernels  17.6 us (37%)
  starting transfers between devices  12.5 us (26%)
  blocking collectives  12.5 us (26%)
  waiting for transfers between devices  3.55 us (7%)
  between operations  0.75 us (2%)
  local copies, waits for them, and re-layouts  0.67 us (1%)
    pallas_call x5, Pallas kernels, call(): pl.pallas_call(kernel, grid=grid, in_specs=in_specs, out_specs=out_specs,...  17.6 us
    all_to_all x1, blocking collectives, on_device(): segments = lax.all_to_all(segment, 'corr', 0, 0)  12.5 us
    ppermute x3, starting transfers between devices, on_device(): lax.ppermute(both, 'lc', [(i, (i + 2 * k) % 8) for i in range(8)])  6.64 us
    ppermute x1, starting transfers between devices, on_device(): lax.ppermute(bwd, 'corr', [((i + 1) % ROWS, i) for i in range(ROWS)])  3.8 us
    ppermute x3, waiting for transfers between devices, on_device(): lax.ppermute(both, 'lc', [(i, (i + 2 * k) % 8) for i in range(8)])  2.17 us
    ppermute x1, starting transfers between devices, on_device(): left = lax.ppermute(fwd, 'corr', [(i, (i + 1) % ROWS) for i in range(ROWS)])  1.57 us
    ppermute x3, waiting for transfers between devices, on_device(): swapped.append(lax.ppermute(pieces[n], 'lc', swap))  1.38 us
  transfers between devices with their start and end apart: 9, of which 4 were waited for; matrix products, arithmetic and copies ran while one was open for 0% of the time, Pallas kernels for 14%

profile of v4, /device:TPU:0, one launch (start us, length us, event | category | flops | bytes accessed | tf_op | source)
XLA Modules:
  0.0 47.6 jit_solution(13508638149511889142)
XLA Ops:
  0.6 0.0 copy-start
  0.6 0.0 copy-start.1
  0.7 0.0 copy-start.2
  0.7 0.0 copy-start.3
  0.7 2.1 %pack.1 = (f32[184,128]{1,0:T(8,128)}, f32[184,128]{1,0:T(8,128)}, f32[304,128]{1,0:T(8,128)}) custom-call(f32[8]{0:T(128)} %cap_table.5, f32[4]{0:T(128)} %jam_table.5, f32[3]{0:T(128)} %coef_ref.7, s32[128]{0:T(128)} %feed_a.1, s32[128]{0:T(128)} %feed_b.1, s32[1,128]{1,0:T(1,128)} %bitcast.12, s32[1,128]{1,0:T(1,128)} %bitcast.13, f32[1,128]{1,0:T(1,128)} %bitcast.14, ...), custom_call_target="tpu_custom_call" | custom-call | bytes 4194304 | tf_op jit(solution)/shard_map/pack/pallas_call | solution.py:727
  2.8 1.6 %collective-permute-start = (f32[184,128]{1,0:T(8,128)}, f32[184,128]{1,0:T(8,128)S(1)}, u32[]{:S(2)}, u32[]{:S(2)}) collective-permute-start(f32[184,128]{1,0:T(8,128)} %get-tuple-element.46), channel_id=1, source_target_pairs={{0,8},{8,16},{16,24},{24,32},{32,40},{40,48},{48,56},{56,64},{64,7... | collective-permute-start | bytes 282632 | tf_op jit(solution)/shard_map/ppermute | solution.py:774
  4.4 3.8 %collective-permute-start.1 = (f32[184,128]{1,0:T(8,128)}, f32[184,128]{1,0:T(8,128)S(1)}, u32[]{:S(2)}, u32[]{:S(2)}) collective-permute-start(f32[184,128]{1,0:T(8,128)} %get-tuple-element.47), channel_id=1, source_target_pairs={{8,0},{16,8},{24,16},{32,24},{40,32},{48,40},{56,48},{64,56},{72,6... | collective-permute-start | bytes 282632 | tf_op jit(solution)/shard_map/ppermute | solution.py:775
  8.2 0.0 copy-start.5
  8.2 0.0 copy-start.6
  8.2 0.0 copy-start.7
  8.2 0.0 copy-done
  8.2 0.0 copy-done.1
  8.2 0.0 copy-done.2
  8.2 0.0 copy-done.3
  8.2 0.6 %copy-done.5 = f32[3]{0:T(128)S(1)} copy-done((f32[3]{0:T(128)S(1)}, f32[3]{0:T(128)}, u32[]{:S(2)}) %copy-start.5) | copy-done | bytes 36
  8.8 0.0 copy-done.6
  8.8 0.0 copy-done.7
  8.9 0.0 copy-start.4
  8.9 3.2 %early.1 = (f32[8,16,8,128]{3,2,1,0:T(8,128)S(1)}, f32[2,8,128]{2,1,0:T(8,128)S(1)}, f32[736,128]{1,0:T(8,128)S(1)}, f32[12,16,8,128]{3,2,1,0:T(8,128)S(1)}, f32...) custom-call(f32[8]{0:T(128)S(1)} %copy-done.6, ...), custom_call_target="tpu_custom_call" | custom-call | flops 67108864 | bytes 4194304 | tf_op jit(solution)/shard_map/early/pallas_call | solution.py:727
  12.0 0.0 collective-permute-done.left
  12.0 0.0 collective-permute-done.1.right
  12.0 0.0 copy-done.4
  12.1 2.0 %collective-permute-start.2 = (f32[304,128]{1,0:T(8,128)S(1)}, f32[304,128]{1,0:T(8,128)S(1)}, u32[]{:S(2)}, u32[]{:S(2)}) collective-permute-start(f32[304,128]{1,0:T(8,128)S(1)} %select_dynamic-update-slice_fusion.e0), channel_id=1, source_target_pairs={{0,2},{1,3},{2,4},{3,5},{4,6},{5,7},{6,0},{7,1},{8,10},{9,11},{10,... | collective-permute-start | bytes 466952 | tf_op jit(solution)/shard_map/ppermute | solution.py:794
  14.1 3.6 %collective-permute-start.3 = (f32[304,128]{1,0:T(8,128)S(1)}, f32[304,128]{1,0:T(8,128)S(1)}, u32[]{:S(2)}, u32[]{:S(2)}) collective-permute-start(f32[304,128]{1,0:T(8,128)S(1)} %select_dynamic-update-slice_fusion.e0), channel_id=1, source_target_pairs={{0,4},{1,5},{2,6},{3,7},{4,0},{5,1},{6,2},{7,3},{8,12},{9,13},{10,... | collective-permute-start | bytes 466952 | tf_op jit(solution)/shard_map/ppermute | solution.py:794
  17.7 1.0 %collective-permute-start.4 = (f32[304,128]{1,0:T(8,128)S(1)}, f32[304,128]{1,0:T(8,128)S(1)}, u32[]{:S(2)}, u32[]{:S(2)}) collective-permute-start(f32[304,128]{1,0:T(8,128)S(1)} %select_dynamic-update-slice_fusion.e0), channel_id=1, source_target_pairs={{0,6},{1,7},{2,0},{3,1},{4,2},{5,3},{6,4},{7,5},{8,14},{9,15},{10,... | collective-permute-start | bytes 466952 | tf_op jit(solution)/shard_map/ppermute | solution.py:794
  18.7 0.0 collective-permute-start.5
  18.7 3.6 %late.1 = (f32[12,128,128]{2,1,0:T(8,128)}, f32[16,8,128]{2,1,0:T(8,128)S(1)}, f32[8,16,8,128]{3,2,1,0:T(8,128)S(1)}, f32[2,8,128]{2,1,0:T(8,128)S(1)}) custom-call(f32[3]{0:T(128)S(1)} %copy-done.5, f32[2,8,128]{2,1,0:T(8,128)S(1)} %get-tuple-element.61.early_stats, f32[12,16,8,128]{3,2,1,0:T(8,128)S(1)} %get-tuple-element.62.st_in, ...), custom_call_target="tpu_custom_call" | custom-call | flops 67108864 | bytes 4194304 | tf_op jit(solution)/shard_map/late/pallas_call | solution.py:727
  22.3 0.0 collective-permute-done.2.e1
  22.3 2.2 %collective-permute-done.3.e2 = f32[304,128]{1,0:T(8,128)S(1)} collective-permute-done((f32[304,128]{1,0:T(8,128)S(1)}, f32[304,128]{1,0:T(8,128)S(1)}, u32[]{:S(2)}, u32[]{:S(2)}) %collective-permute-start.3) | collective-permute-done | bytes 155680 | tf_op jit(solution)/shard_map/ppermute | solution.py:794
  24.4 0.0 collective-permute-done.4.e3
  24.4 0.0 collective-permute-start.8
  24.4 0.5 %collective-permute-start.7 = (f32[304,128]{1,0:T(8,128)S(1)}, f32[304,128]{1,0:T(8,128)S(1)}, u32[]{:S(2)}, u32[]{:S(2)}) collective-permute-start(f32[304,128]{1,0:T(8,128)S(1)} %collective-permute-done.3.e2), channel_id=1, source_target_pairs={{0,1},{1,0},{2,3},{3,2},{4,5},{5,4},{6,7},{7,6},{8,9},{9,8},{10,11... | collective-permute-start | bytes 466952 | tf_op jit(solution)/shard_map/ppermute | solution.py:808
  25.0 0.0 collective-permute-start.6
  25.0 0.0 collective-permute-done.5.e4
  25.0 0.9 %collective-permute-done.8.e7 = f32[304,128]{1,0:T(8,128)S(1)} collective-permute-done((f32[304,128]{1,0:T(8,128)S(1)}, f32[304,128]{1,0:T(8,128)S(1)}, u32[]{:S(2)}, u32[]{:S(2)}) %collective-permute-start.8) | collective-permute-done | bytes 155680 | tf_op jit(solution)/shard_map/ppermute | solution.py:808
  25.8 0.2 collective-permute-done.7.e6
  26.1 0.3 collective-permute-done.6.e5
  26.3 7.5 %edges.1 = (f32[2,12,8,128]{3,2,1,0:T(8,128)S(1)}, f32[16,2,8,128]{3,2,1,0:T(8,128)S(1)}, f32[4,8,128]{2,1,0:T(8,128)S(1)}, f32[6,8,128]{2,1,0:T(8,128)S(1)}, f32[8,6,8,128]{3,2,1,0:T(8,128)S(1)}) custom-call(f32[8]{0:T(128)S(1)} %copy-done.6, f32[4]{0:T(128)S(1)} %copy-done.7, f32[3]{0:T(128)S(1)} %copy-done.5, f32[736,128]{1,0:T(8,128)S(1)} %get-tuple-element.45.strip, ...), custom_call_target="tpu_custom_call" | custom-call | bytes 4194304 | tf_op jit(solution)/shard_map/edges/pallas_call | solution.py:727
  33.9 12.5 %all_to_all.5.segments = f32[16,2,8,128]{3,2,1,0:T(8,128)S(1)} all-to-all(f32[16,2,8,128]{3,2,1,0:T(8,128)S(1)} %get-tuple-element.77), channel_id=1, replica_groups=mesh['corr'=16,'lc'=8] {'corr'}, dimensions={0} | all-to-all | bytes 262144 | tf_op jit(solution)/shard_map/all_to_all | solution.py:824
  46.4 1.3 %count.1 = (f32[128,128]{1,0:T(8,128)}, f32[12,128,128]{2,1,0:T(8,128)}) custom-call(f32[16,2,8,128]{3,2,1,0:T(8,128)S(1)} %all_to_all.5.segments, f32[4,8,128]{2,1,0:T(8,128)S(1)} %get-tuple-element.78.aux, f32[2,8,128]{2,1,0:T(8,128)S(1)} %get-tuple-element.76.inner, f32[16,8,128]{2,1,0:T(8,128)S(1)} %get-tuple-element.79.acc, ...), custom_call_target="tpu_custom_call", output_to_operand_aliasing={{1}: (9, {})} | custom-call | bytes 4194304 | tf_op jit(solution)/shard_map/count/pallas_call | solution.py:727
  (1 shorter events, 0.0 us)
Async XLA Ops:
  0.6 7.5 %copy-start = (f32[4,3,128,128]{3,2,1,0:T(8,128)S(1)}, f32[4,3,128,128]{3,2,1,0:T(8,128)}, u32[]{:S(2)}) copy-start(f32[4,3,128,128]{3,2,1,0:T(8,128)} %param.12) | copy-start | bytes 2359300
  0.6 7.5 %copy-start.1 = (s32[4,128,128]{2,1,0:T(8,128)S(1)}, s32[4,128,128]{2,1,0:T(8,128)}, u32[]{:S(2)}) copy-start(s32[4,128,128]{2,1,0:T(8,128)} %c_hi.1) | copy-start | bytes 786436
  0.7 7.5 %copy-start.2 = (s32[4,128,128]{2,1,0:T(8,128)S(1)}, s32[4,128,128]{2,1,0:T(8,128)}, u32[]{:S(2)}) copy-start(s32[4,128,128]{2,1,0:T(8,128)} %j_hi.1) | copy-start | bytes 786436
  0.7 7.5 %copy-start.3 = (s32[3,128,128]{2,1,0:T(8,128)S(1)}, s32[3,128,128]{2,1,0:T(8,128)}, u32[]{:S(2)}) copy-start(s32[3,128,128]{2,1,0:T(8,128)} %a_hi.1) | copy-start | bytes 589828
  2.8 9.2 %collective-permute-start = (f32[184,128]{1,0:T(8,128)}, f32[184,128]{1,0:T(8,128)S(1)}, u32[]{:S(2)}, u32[]{:S(2)}) collective-permute-start(f32[184,128]{1,0:T(8,128)} %get-tuple-element.46), channel_id=1, source_target_pairs={{0,8},{8,16},{16,24},{24,32},{32,40},{40,48},{48,56},{56,64},{64,7... | collective-permute-start | bytes 282632 | tf_op jit(solution)/shard_map/ppermute | solution.py:774
  4.4 7.7 %collective-permute-start.1 = (f32[184,128]{1,0:T(8,128)}, f32[184,128]{1,0:T(8,128)S(1)}, u32[]{:S(2)}, u32[]{:S(2)}) collective-permute-start(f32[184,128]{1,0:T(8,128)} %get-tuple-element.47), channel_id=1, source_target_pairs={{8,0},{16,8},{24,16},{32,24},{40,32},{48,40},{56,48},{64,56},{72,6... | collective-permute-start | bytes 282632 | tf_op jit(solution)/shard_map/ppermute | solution.py:775
  8.2 0.7 %copy-start.5 = (f32[3]{0:T(128)S(1)}, f32[3]{0:T(128)}, u32[]{:S(2)}) copy-start(f32[3]{0:T(128)} %coef_ref.7) | copy-start | bytes 40
  8.2 0.7 %copy-start.6 = (f32[8]{0:T(128)S(1)}, f32[8]{0:T(128)}, u32[]{:S(2)}) copy-start(f32[8]{0:T(128)} %cap_table.5) | copy-start | bytes 100
  8.2 0.7 %copy-start.7 = (f32[4]{0:T(128)S(1)}, f32[4]{0:T(128)}, u32[]{:S(2)}) copy-start(f32[4]{0:T(128)} %jam_table.5) | copy-start | bytes 52
  8.9 3.2 %copy-start.4 = (f32[304,128]{1,0:T(8,128)S(1)}, f32[304,128]{1,0:T(8,128)}, u32[]{:S(2)}) copy-start(f32[304,128]{1,0:T(8,128)} %get-tuple-element.51) | copy-start | bytes 466948
  12.1 10.2 %collective-permute-start.2 = (f32[304,128]{1,0:T(8,128)S(1)}, f32[304,128]{1,0:T(8,128)S(1)}, u32[]{:S(2)}, u32[]{:S(2)}) collective-permute-start(f32[304,128]{1,0:T(8,128)S(1)} %select_dynamic-update-slice_fusion.e0), channel_id=1, source_target_pairs={{0,2},{1,3},{2,4},{3,5},{4,6},{5,7},{6,0},{7,1},{8,10},{9,11},{10,... | collective-permute-start | bytes 466952 | tf_op jit(solution)/shard_map/ppermute | solution.py:794
  14.1 10.3 %collective-permute-start.3 = (f32[304,128]{1,0:T(8,128)S(1)}, f32[304,128]{1,0:T(8,128)S(1)}, u32[]{:S(2)}, u32[]{:S(2)}) collective-permute-start(f32[304,128]{1,0:T(8,128)S(1)} %select_dynamic-update-slice_fusion.e0), channel_id=1, source_target_pairs={{0,4},{1,5},{2,6},{3,7},{4,0},{5,1},{6,2},{7,3},{8,12},{9,13},{10,... | collective-permute-start | bytes 466952 | tf_op jit(solution)/shard_map/ppermute | solution.py:794
  17.7 6.7 %collective-permute-start.4 = (f32[304,128]{1,0:T(8,128)S(1)}, f32[304,128]{1,0:T(8,128)S(1)}, u32[]{:S(2)}, u32[]{:S(2)}) collective-permute-start(f32[304,128]{1,0:T(8,128)S(1)} %select_dynamic-update-slice_fusion.e0), channel_id=1, source_target_pairs={{0,6},{1,7},{2,0},{3,1},{4,2},{5,3},{6,4},{7,5},{8,14},{9,15},{10,... | collective-permute-start | bytes 466952 | tf_op jit(solution)/shard_map/ppermute | solution.py:794
  18.7 6.2 %collective-permute-start.5 = (f32[304,128]{1,0:T(8,128)S(1)}, f32[304,128]{1,0:T(8,128)S(1)}, u32[]{:S(2)}, u32[]{:S(2)}) collective-permute-start(f32[304,128]{1,0:T(8,128)S(1)} %select_dynamic-update-slice_fusion.e0), channel_id=1, source_target_pairs={{0,1},{1,0},{2,3},{3,2},{4,5},{5,4},{6,7},{7,6},{8,9},{9,8},{10,11... | collective-permute-start | bytes 466952 | tf_op jit(solution)/shard_map/ppermute | solution.py:805
  24.4 1.4 %collective-permute-start.8 = (f32[304,128]{1,0:T(8,128)S(1)}, f32[304,128]{1,0:T(8,128)S(1)}, u32[]{:S(2)}, u32[]{:S(2)}) collective-permute-start(f32[304,128]{1,0:T(8,128)S(1)} %collective-permute-done.4.e3), channel_id=1, source_target_pairs={{0,1},{1,0},{2,3},{3,2},{4,5},{5,4},{6,7},{7,6},{8,9},{9,8},{10,11... | collective-permute-start | bytes 466952 | tf_op jit(solution)/shard_map/ppermute | solution.py:808
  24.4 1.6 %collective-permute-start.7 = (f32[304,128]{1,0:T(8,128)S(1)}, f32[304,128]{1,0:T(8,128)S(1)}, u32[]{:S(2)}, u32[]{:S(2)}) collective-permute-start(f32[304,128]{1,0:T(8,128)S(1)} %collective-permute-done.3.e2), channel_id=1, source_target_pairs={{0,1},{1,0},{2,3},{3,2},{4,5},{5,4},{6,7},{7,6},{8,9},{9,8},{10,11... | collective-permute-start | bytes 466952 | tf_op jit(solution)/shard_map/ppermute | solution.py:808
  25.0 1.4 %collective-permute-start.6 = (f32[304,128]{1,0:T(8,128)S(1)}, f32[304,128]{1,0:T(8,128)S(1)}, u32[]{:S(2)}, u32[]{:S(2)}) collective-permute-start(f32[304,128]{1,0:T(8,128)S(1)} %collective-permute-done.2.e1), channel_id=1, source_target_pairs={{0,1},{1,0},{2,3},{3,2},{4,5},{5,4},{6,7},{7,6},{8,9},{9,8},{10,11... | collective-permute-start | bytes 466952 | tf_op jit(solution)/shard_map/ppermute | solution.py:808
